TPU v7x, 512 devices: a whole 4x8x8 slice. The times are simulated.
512 devices in a mesh: tm: 64 (over y, x, core), gz: 8 (over z).
Axes of the slice: x: 4, y: 8, z: 8, core: 2. Of those that a mesh axis runs over, the one named last changes fastest.
Arguments:
- cpoint_guess: float32 [64, 32, 32, 128], P('tm', 'gz'), may hold values from -1 to 1
- initial_state: float32 [32, 32, 128], P('gz'), may hold values from -1 to 1
- diffusivity: float32 [32, 32, 128], P('gz'), may hold values from 0.05 to 1
- growth_rate: float32 [32, 32, 128], P('gz'), may hold values from 0.5 to 2
Outputs:
- corrected: float32 [64, 32, 32, 128], P('tm', 'gz')
- residual: float32 [64, 32, 32, 128], P('tm', 'gz')
All inputs are finite; a program needn't handle non-finite values.
Results may differ from a plain program's by a relative error of at most 0.00002.
Values sent between devices are 32-bit elements; how exact they have to be, the bound alone decides.
No kernel may reach another device: no remote copies, remote signals or barrier semaphores. Data moves between devices by JAX's collectives and lax.ppermute only.
A program may use at most 64 MiB of HBM per device.

v0:
```python
import jax
import jax.numpy as jnp
from jax import lax
from jax.sharding import PartitionSpec as P

STEPS = 8


FINE_STEP = 0.01875


def with_halo(block, sides, width):
    for axis, dim in sides:
        count = lax.axis_size(axis)
        forward = [(i, i + 1) for i in range(count - 1)]
        backward = [(target, source) for source, target in forward]
        low = lax.ppermute(
            lax.slice_in_dim(block, block.shape[dim] - width, None, axis=dim), axis, forward
        )
        high = lax.ppermute(lax.slice_in_dim(block, 0, width, axis=dim), axis, backward)
        block = jnp.concatenate([low, block, high], axis=dim)
    return block


def shifted(value, axis, steps):
    count = lax.axis_size(axis)
    leading, last = (max(0, -steps), min(count, count - steps))
    return lax.ppermute(value, axis, [(source, source + steps) for source in range(leading, last)])


def advance(extended, kappa_ext, growth_mid, time_step):
    center = extended[..., 1:-1, :, :]
    kappa_mid = kappa_ext[..., 1:-1, :, :]
    widths = [(0, 0)] * (center.ndim - 2) + [(1, 1), (1, 1)]
    kappa_widths = [(0, 0)] * (kappa_mid.ndim - 2) + [(1, 1), (1, 1)]
    padded = jnp.pad(center, widths)
    kappa_pad = jnp.pad(kappa_mid, kappa_widths)
    neighbours = [
        (extended[..., 2:, :, :], kappa_ext[..., 2:, :, :]),
        (extended[..., :-2, :, :], kappa_ext[..., :-2, :, :]),
        (padded[..., :, 2:, 1:-1], kappa_pad[..., :, 2:, 1:-1]),
        (padded[..., :, :-2, 1:-1], kappa_pad[..., :, :-2, 1:-1]),
        (padded[..., :, 1:-1, 2:], kappa_pad[..., :, 1:-1, 2:]),
        (padded[..., :, 1:-1, :-2], kappa_pad[..., :, 1:-1, :-2]),
    ]
    flux_sum = jnp.zeros_like(center)
    for values, kappas in neighbours:
        flux_sum = flux_sum + 0.5 * (kappas + kappa_mid) * (values - center)
    reaction = growth_mid * (center - center * center * center)
    return center + time_step * (flux_sum + reaction)


def shards(cpoint_guess, initial_state, diffusivity, growth_rate):
    time_rank = lax.axis_index("tm")
    slab_depth = diffusivity.shape[0]
    intervals = lax.axis_size("tm")
    coef_ext = with_halo(jnp.stack([diffusivity, growth_rate]), (("gz", 1),), 4)
    kappa_one = coef_ext[0, 3 : slab_depth + 5]

    def shift_prev(states):
        arrived = shifted(states, "tm", 1)
        return jnp.where(time_rank == 0, initial_state, arrived)

    def coarse_step(states):
        extended = with_halo(states, (("gz", 0),), 1)
        return advance(extended, kappa_one, growth_rate, FINE_STEP * STEPS)

    def propagate(states):
        for substep in range(STEPS):
            extended = with_halo(states, (("gz", 0),), 1)
            states = advance(extended, kappa_one, growth_rate, FINE_STEP)
        return states

    opening = shift_prev(cpoint_guess[0])
    relaxed = propagate(opening)
    restart = shift_prev(relaxed)
    reached = propagate(restart)
    residual = reached - relaxed
    forcing = reached - coarse_step(restart)
    zeroed = jnp.zeros_like(initial_state)

    def relay_step(number, carried):
        incoming, result = carried
        current = coarse_step(incoming) + forcing
        result = jnp.where(number == time_rank, current, result)
        incoming = shifted(current, "tm", 1)
        return (incoming, result)

    starting = jnp.where(time_rank == 0, initial_state, 0.0)
    incoming, result = lax.fori_loop(0, intervals - 1, relay_step, (starting, zeroed))
    current = coarse_step(incoming) + forcing
    corrected = jnp.where(time_rank == intervals - 1, current, result)
    return (corrected[None], residual[None])


def solution(mesh):
    in_specs = (
        P("tm", "gz", None, None),
        P("gz", None, None),
        P("gz", None, None),
        P("gz", None, None),
    )
    out_specs = (P("tm", "gz", None, None), P("tm", "gz", None, None))
    return jax.shard_map(shards, mesh=mesh, in_specs=in_specs, out_specs=out_specs, check_vma=False)
```

profile of v0, /device:TPU:32, one launch (start us, length us, event | category | flops | bytes accessed | tf_op | source)
XLA Modules:
  0.0 1300.9 jit_solution(13776137157588659214)
XLA Ops:
  80.6 7.0 collective-permute-done.22
  159.4 1133.4 %while.18 = (s32[]{:T(128)}, f32[4,32,128]{2,1,0:T(8,128)S(1)}, f32[4,32,128]{2,1,0:T(8,128)S(1)}, f32[4,32,128]{2,1,0:T(8,128)S(1)}, f32[4,32,128]{2,1,0:T(8,12...) while((s32[]{:T(128)}, f32[4,32,128]{2,1,0:T(8,128)S(1)}, ...), condition=%wide.region_1.2_spmd.clone, body=%wide.region_0.1_spmd.clone.sunk | while | flops 638980 | bytes 1212665 | solution.py:90
  195.7 7.0 collective-permute-done.2
  215.5 7.0 collective-permute-done.2
  234.1 7.0 collective-permute-done.2
  251.9 7.0 collective-permute-done.2
  269.8 7.0 collective-permute-done.2
  323.2 7.0 collective-permute-done.2
  341.1 7.0 collective-permute-done.2
  358.9 7.0 collective-permute-done.2
  412.4 7.0 collective-permute-done.2
  430.2 7.0 collective-permute-done.2
  483.7 7.0 collective-permute-done.2
  501.5 7.0 collective-permute-done.2
  519.3 7.0 collective-permute-done.2
  572.8 7.0 collective-permute-done.2
  590.6 7.0 collective-permute-done.2
  608.5 7.0 collective-permute-done.2
  661.9 7.0 collective-permute-done.2
  679.8 7.0 collective-permute-done.2
  697.6 7.0 collective-permute-done.2
  751.1 7.0 collective-permute-done.2
  768.9 7.0 collective-permute-done.2
  822.4 7.0 collective-permute-done.2
  840.2 7.0 collective-permute-done.2
  858.0 7.0 collective-permute-done.2
  911.5 7.0 collective-permute-done.2
  929.3 7.0 collective-permute-done.2
  947.2 7.0 collective-permute-done.2
  1000.6 7.0 collective-permute-done.2
  1018.5 7.0 collective-permute-done.2
  1036.3 7.0 collective-permute-done.2
  (658 shorter events, 1080.0 us)
Async XLA Ops:
  0.6 9.1 collective-permute-start.5
  3.5 14.1 %collective-permute-start.3 = (f32[2,4,32,128]{3,2,1,0:T(8,128)S(1)}, f32[2,4,32,128]{3,2,1,0:T(8,128)S(1)}, u32[]{:S(2)}, u32[]{:S(2)}) collective-permute-start(f32[2,4,32,128]{3,2,1,0:T(8,128)S(1)} %pad_maximum_fusion.2), channel_id=1, source_target_pairs={{1,0},{2,1},{3,2},{4,3},{5,4},{6,5},{7,6},{9,8},{10,9},{11,10},{12... | collective-permute-start | bytes 393224 | tf_op jit(solution)/shard_map/ppermute | solution.py:20
  4.8 12.8 collective-permute-start.4
  172.1 8.9 collective-permute-start.2
  193.7 8.9 collective-permute-start.2
  213.6 8.9 collective-permute-start.2
  232.2 8.9 collective-permute-start.2
  250.0 8.9 collective-permute-start.2
  267.8 8.9 collective-permute-start.2
  303.5 8.9 collective-permute-start.2
  321.3 8.9 collective-permute-start.2
  339.1 8.9 collective-permute-start.2
  357.0 8.9 collective-permute-start.2
  374.8 8.9 collective-permute-start.2
  392.6 8.9 collective-permute-start.2
  410.4 8.9 collective-permute-start.2
  428.3 8.9 collective-permute-start.2
  463.9 8.9 collective-permute-start.2
  481.8 8.9 collective-permute-start.2
  499.6 8.9 collective-permute-start.2
  517.4 8.9 collective-permute-start.2
  553.1 8.9 collective-permute-start.2
  570.9 8.9 collective-permute-start.2
  588.7 8.9 collective-permute-start.2
  606.5 8.9 collective-permute-start.2
  642.2 8.9 collective-permute-start.2
  660.0 8.9 collective-permute-start.2
  677.8 8.9 collective-permute-start.2
  695.7 8.9 collective-permute-start.2
  713.5 8.9 collective-permute-start.2
  731.3 8.9 collective-permute-start.2
  749.1 8.9 collective-permute-start.2
  (198 other events, 1230.6 us)
where the time goes:
time: 1310 us; the launch traced here: 1300 us
  waiting for transfers between devices  745 us (57%)
  starting transfers between devices  537 us (41%)
  other arithmetic  13.5 us (1%)
    ppermute x65, waiting for transfers between devices, shifted(): lax.ppermute(value, axis, [(source, source + steps) for source in range(l...  446 us
    ppermute x81, starting transfers between devices, with_halo(): lax.ppermute(lax.slice_in_dim(block, block.shape[dim] - width, None, axis...  307 us
    ppermute x81, waiting for transfers between devices, with_halo(): lax.ppermute(lax.slice_in_dim(block, 0, width, axis=dim), axis, backward)  268 us
    ppermute x65, starting transfers between devices, shifted(): lax.ppermute(value, axis, [(source, source + steps) for source in range(l...  125 us
    ppermute x81, starting transfers between devices, with_halo(): lax.ppermute(lax.slice_in_dim(block, 0, width, axis=dim), axis, backward)  105 us
    ppermute x81, waiting for transfers between devices, with_halo(): lax.ppermute(lax.slice_in_dim(block, block.shape[dim] - width, None, axis...  30.6 us
  transfers between devices with their start and end apart: 227, of which 207 were waited for; matrix products, arithmetic and copies ran while one was open for 0% of the time, Pallas kernels for 0%

commit v1 on v0

v1 whole, which is shorter than its diff:
```python
import functools

import jax
import jax.numpy as jnp
from jax import lax
from jax.experimental import pallas as pl
from jax.experimental.pallas import tpu as pltpu
from jax.sharding import PartitionSpec as P

STEPS = 8
FINE_STEP = 0.01875
COARSE_STEP = FINE_STEP * STEPS
NZ, NX, NY = 32, 32, 128
SLAB = 4
HALF = NZ // 2
UNROLL = 4
ROW = 8
VMEM_BYTES = 52 * 1024 * 1024

PLANE = (NX, NY)
PADDED = (NZ + 2, NX + 16, NY)
COEFS = 7


def scratch_set():
    full = pltpu.VMEM((NZ, *PLANE), jnp.float32)
    return [
        pltpu.VMEM(PADDED, jnp.float32),
        pltpu.VMEM(PADDED, jnp.float32),
        pltpu.VMEM((NZ + 1, *PLANE), jnp.float32),
        full,
        full,
        full,
        full,
        full,
        full,
    ]


def put(ref, z, value):
    ref[z + 1, ROW : ROW + NX, :] = value


def get(ref, z):
    return ref[z + 1, ROW : ROW + NX, :]


def clear_edges(ref):
    ref[0] = jnp.zeros(PADDED[1:], jnp.float32)
    ref[NZ + 1] = jnp.zeros(PADDED[1:], jnp.float32)

    def body(z, carry):
        ref[z + 1, 0:ROW, :] = jnp.zeros((ROW, NY), jnp.float32)
        ref[z + 1, ROW + NX : 2 * ROW + NX, :] = jnp.zeros((ROW, NY), jnp.float32)
        return carry

    lax.fori_loop(0, NZ, body, 0)


def build(a, coefs, kappa, growth, h):
    az, axm, axp, aym, ayp, diag, react = coefs
    half_h = 0.5 * h
    for z in range(NZ):
        put(a, z, kappa(z))
    lane = lax.broadcasted_iota(jnp.int32, PLANE, 1)

    az[0] = half_h * get(a, 0)

    def body(z, carry):
        k = get(a, z)
        up = half_h * (a[z + 2, ROW : ROW + NX, :] + k)
        down = half_h * (a[z, ROW : ROW + NX, :] + k)
        xm = half_h * (a[z + 1, ROW - 1 : ROW - 1 + NX, :] + k)
        xp = half_h * (a[z + 1, ROW + 1 : ROW + 1 + NX, :] + k)
        ym = half_h * (jnp.where(lane == 0, 0.0, pltpu.roll(k, 1, 1)) + k)
        yp = half_h * (jnp.where(lane == NY - 1, 0.0, pltpu.roll(k, NY - 1, 1)) + k)
        az[z + 1] = up
        axm[z] = xm
        axp[z] = xp
        aym[z] = jnp.where(lane == 0, 0.0, ym)
        ayp[z] = jnp.where(lane == NY - 1, 0.0, yp)
        hr = react[z]
        diag[z] = 1.0 + hr - (up + down + xm + xp + ym + yp)
        return carry

    for z in range(NZ):
        react[z] = h * growth(z)
    lax.fori_loop(0, NZ, body, 0)


def rescale(coefs, factor):
    def body(z, carry):
        for ref in coefs[:5] + coefs[6:]:
            ref[z] = factor * ref[z]
        coefs[5][z] = 1.0 + factor * (coefs[5][z] - 1.0)
        return carry

    lax.fori_loop(0, NZ, body, 0)
    coefs[0][NZ] = factor * coefs[0][NZ]


def step(src, dst, coefs, finish=None):
    az, axm, axp, aym, ayp, diag, react = coefs

    def chunk(i, carry):
        base = i * UNROLL
        below = src[base, ROW : ROW + NX, :]
        here = src[base + 1, ROW : ROW + NX, :]
        face = az[base]
        for j in range(UNROLL):
            z = base + j
            above = src[z + 2, ROW : ROW + NX, :]
            next_face = az[z + 1]
            value = here * (diag[z] - react[z] * (here * here))
            value = value + (face * below + next_face * above)
            value = value + (
                axm[z] * src[z + 1, ROW - 1 : ROW - 1 + NX, :]
                + axp[z] * src[z + 1, ROW + 1 : ROW + 1 + NX, :]
            )
            value = value + (aym[z] * pltpu.roll(here, 1, 1) + ayp[z] * pltpu.roll(here, NY - 1, 1))
            if finish is not None:
                value = finish(z, value)
            dst[z + 1, ROW : ROW + NX, :] = value
            below, here, face = here, above, next_face
        return carry

    lax.fori_loop(0, NZ // UNROLL, chunk, 0)


def fine(a, b, coefs):
    def pair(i, carry):
        step(a, b, coefs)
        step(b, a, coefs)
        return carry

    lax.fori_loop(0, STEPS // 2, pair, 0)


def copy_slab(src, first, out):
    for i in range(SLAB):
        out[i] = get(src, first + i)


def copy_state(src, dst):
    def body(z, carry):
        put(dst, z, get(src, z))
        return carry

    lax.fori_loop(0, NZ, body, 0)


def copy_out(src, out):
    def body(z, carry):
        out[z] = get(src, z)
        return carry

    lax.fori_loop(0, NZ, body, 0)


def field(gathered, number):
    return lambda z: gathered[z // SLAB, number, z % SLAB]


def fine_kernel(where, gathered, keep, send, u_out, w_out, a, b, *coefs):
    first = where[0] * SLAB
    core = where[1]
    clear_edges(a)
    clear_edges(b)
    build(a, coefs, field(gathered, 1), field(gathered, 2), FINE_STEP)
    for z in range(NZ):
        put(a, z, gathered[z // SLAB, 0, z % SLAB])
    fine(a, b, coefs)
    copy_slab(a, first, u_out)

    def save(z, carry):
        keep[z] = get(a, core * HALF + z)
        send[z] = get(a, (1 - core) * HALF + z)
        return carry

    lax.fori_loop(0, HALF, save, 0)
    fine(a, b, coefs)
    copy_slab(a, first, w_out)

    def restore(z, carry):
        put(b, core * HALF + z, keep[z])
        put(b, (1 - core) * HALF + z, send[z])
        return carry

    lax.fori_loop(0, HALF, restore, 0)
    rescale(coefs, float(STEPS))
    step(b, a, coefs, finish=lambda z, value: get(a, z) - value)

    def emit(z, carry):
        keep[z] = get(a, core * HALF + z)
        send[z] = get(a, (1 - core) * HALF + z)
        return carry

    lax.fori_loop(0, HALF, emit, 0)


def start_kernel(where, gathered, state_out, slabs, a, b, c, *coefs):
    first = where[0] * SLAB
    clear_edges(a)
    clear_edges(b)
    clear_edges(c)
    build(a, coefs, field(gathered, 1), field(gathered, 2), FINE_STEP)
    for z in range(NZ):
        put(a, z, gathered[z // SLAB, 3, z % SLAB])
    fine(a, b, coefs)
    copy_state(a, c)
    copy_slab(a, first, slabs.at[0])
    fine(a, b, coefs)
    copy_slab(a, first, slabs.at[1])
    rescale(coefs, float(STEPS))
    step(c, b, coefs, finish=lambda z, value: get(a, z) - value)

    copy_out(b, state_out)
    for z in range(NZ):
        put(a, z, gathered[z // SLAB, 3, z % SLAB])
    step(a, b, coefs, finish=lambda z, value: value + (get(c, z) - value))
    copy_slab(b, first, slabs.at[2])
    step(b, a, coefs, finish=lambda z, value: value + state_out[z])
    copy_slab(a, first, slabs.at[3])
    copy_out(a, state_out)


def chain_kernel(counts, halves, *refs):
    where, gathered, state = refs[0], refs[1], refs[2]
    at = 3
    if halves:
        state_other = refs[3]
        at = 4
    segments = refs[at : at + 2 * len(counts)]
    at += 2 * len(counts)
    state_out, picked, late, forcing, sems, a, b = refs[at : at + 7]
    coefs = refs[at + 7 :]
    first = where[0] * SLAB
    core = where[1]
    target = where[2]
    chips = sum(counts)

    def copies(chip):
        done = 0
        found = []
        for number, count in enumerate(counts):
            found.append((done, done + count, segments[2 * number], segments[2 * number + 1]))
            done += count
        return found

    def copy_of(source, q, chip, slot, side):
        parity = jnp.where(side == 0, core, 1 - core)
        half = parity
        real = slot ^ parity
        return pltpu.make_async_copy(
            source.at[q, real],
            forcing.at[2 * chip + slot, pl.ds(half * HALF, HALF)],
            sems.at[2 * chip + slot, side],
        )

    for low, high, own, other in copies(0):

        def launch(chip, carry, low=low, own=own, other=other):
            for slot in range(2):
                copy_of(own, chip - low, chip, slot, 0).start()
                copy_of(other, chip - low, chip, slot, 1).start()
            return carry

        lax.fori_loop(low, high, launch, 0)

    clear_edges(a)
    clear_edges(b)
    build(a, coefs, field(gathered, 1), field(gathered, 2), COARSE_STEP)

    if halves:

        def load(z, carry):
            put(a, core * HALF + z, state[z])
            put(a, (1 - core) * HALF + z, state_other[z])
            return carry

        lax.fori_loop(0, HALF, load, 0)
    else:

        def load(z, carry):
            put(a, z, state[z])
            return carry

        lax.fori_loop(0, NZ, load, 0)

    copy_slab(a, first, picked)

    def advance(src, dst, chip, slot):
        for side in range(2):
            copy_of(segments[0], 0, chip, slot, side).wait()
        index = 2 * chip + slot
        step(src, dst, coefs, finish=lambda z, value: value + forcing[index, z])

        @pl.when(index == target)
        def _():
            copy_slab(dst, first, picked)

    def pair(chip, carry):
        advance(a, b, chip, 0)
        advance(b, a, chip, 1)
        return carry

    lax.fori_loop(0, chips, pair, 0)
    copy_slab(b, first, late)

    if state_out.shape[0] == NZ:
        copy_out(a, state_out)
    else:

        def out(z, carry):
            state_out[z] = get(a, core * HALF + z)
            return carry

        lax.fori_loop(0, HALF, out, 0)


def params():
    return pltpu.CompilerParams(vmem_limit_bytes=VMEM_BYTES)


def cost(steps):
    cells = NZ * NX * NY
    return pl.CostEstimate(flops=18 * cells * steps, bytes_accessed=4 * 10 * cells * steps, transcendentals=0)


VMEM_SPEC = pl.BlockSpec(memory_space=pltpu.VMEM)
SMEM_SPEC = pl.BlockSpec(memory_space=pltpu.SMEM)
ANY_SPEC = pl.BlockSpec(memory_space=pl.ANY)


def f32(*shape):
    return jax.ShapeDtypeStruct(shape, jnp.float32)


def run_fine(where, gathered):
    return pl.pallas_call(
        fine_kernel,
        out_shape=[f32(HALF, *PLANE), f32(HALF, *PLANE), f32(SLAB, *PLANE), f32(SLAB, *PLANE)],
        in_specs=[SMEM_SPEC, VMEM_SPEC],
        out_specs=[VMEM_SPEC] * 4,
        scratch_shapes=scratch_set(),
        compiler_params=params(),
        cost_estimate=cost(18),
    )(where, gathered)


def run_start(where, gathered):
    return pl.pallas_call(
        start_kernel,
        out_shape=[f32(NZ, *PLANE), f32(4, SLAB, *PLANE)],
        in_specs=[SMEM_SPEC, VMEM_SPEC],
        out_specs=[VMEM_SPEC] * 2,
        scratch_shapes=[pltpu.VMEM(PADDED, jnp.float32)] + scratch_set(),
        compiler_params=params(),
        cost_estimate=cost(20),
    )(where, gathered)


def run_chain(where, gathered, states, segments, planes_out):
    counts = tuple(own.shape[0] for own, _ in segments)
    halves = len(states) == 2
    chips = sum(counts)
    arrays = [array for segment in segments for array in segment]
    return pl.pallas_call(
        functools.partial(chain_kernel, counts, halves),
        out_shape=[f32(planes_out, *PLANE), f32(SLAB, *PLANE), f32(SLAB, *PLANE)],
        in_specs=[SMEM_SPEC, VMEM_SPEC] + [VMEM_SPEC] * len(states) + [ANY_SPEC] * len(arrays),
        out_specs=[VMEM_SPEC] * 3,
        scratch_shapes=[
            pltpu.VMEM((2 * chips, NZ, *PLANE), jnp.float32),
            pltpu.SemaphoreType.DMA((2 * chips, 2)),
        ]
        + scratch_set(),
        compiler_params=params(),
        cost_estimate=cost(2 * chips),
    )(where, gathered, *states, *arrays)


def shards(cpoint_guess, initial_state, diffusivity, growth_rate):
    rank = lax.axis_index("tm")
    z_rank = lax.axis_index("gz")
    count = lax.axis_size("tm")
    core = rank % 2
    part = count // 2
    swap = [(i, i ^ 1) for i in range(count)]

    with jax.named_scope("gather_fields"):
        fields = jnp.stack([cpoint_guess[0], diffusivity, growth_rate, initial_state])
        gathered = lax.all_gather(fields, "gz")

    where = jnp.stack([z_rank, core, z_rank]).astype(jnp.int32)
    with jax.named_scope("fine_spans"):
        keep, send, u_slab, w_slab = run_fine(where, gathered)
    with jax.named_scope("forcing_halves"):
        arrived = lax.ppermute(send, "tm", swap)
        mine = jnp.stack([keep, arrived])
    with jax.named_scope("gather_forcing"):
        groups = [[part * g + 2 * q + c for q in range(part // 2)] for g in range(2) for c in range(2)]
        own = lax.all_gather(mine, "tm", axis_index_groups=groups)
    with jax.named_scope("first_intervals"):
        state, slabs = run_start(where, gathered)
    with jax.named_scope("residual"):
        u_prev = lax.ppermute(u_slab, "tm", [(i, i + 1) for i in range(count - 1)])
        w_prev = lax.ppermute(w_slab, "tm", [(i, i + 2) for i in range(count - 2)])
        reached = jnp.where(rank == 0, slabs[0], jnp.where(rank == 1, slabs[1], w_prev))
        relaxed = jnp.where(rank == 0, slabs[0], u_prev)
        residual = reached - relaxed

    lead = 4
    with jax.named_scope("swap_forcing"):
        own_a, own_b = own[:lead], own[lead:]
        other_a = lax.ppermute(own_a, "tm", swap)
        other_b = lax.ppermute(own_b, "tm", swap)

    def where_for(target):
        return jnp.stack([z_rank, core, target]).astype(jnp.int32)

    with jax.named_scope("first_chain"):
        state, picked_a, _ = run_chain(where_for(rank - 2), gathered, [state], [(own_a, other_a)], NZ)
        half, picked_b, late = run_chain(
            where_for(rank - 2 - 2 * lead), gathered, [state], [(own_b, other_b)], HALF
        )
    with jax.named_scope("hand_over"):
        row = 8
        rows = count // row
        pairs = [
            (y * row + i, (rows - 1 - y) * row + i) for y in range(rows // 2) for i in range(row)
        ]
        half = lax.ppermute(half, "tm", pairs)
        other_half = lax.ppermute(half, "tm", swap)
        late = lax.ppermute(late, "tm", [(part - row, part)])
    with jax.named_scope("second_chain"):
        _, picked_c, _ = run_chain(
            where_for(rank - part - 2), gathered, [half, other_half], [(own_a, other_a), (own_b, other_b)], HALF
        )
    with jax.named_scope("corrected"):
        corrected = jnp.where(rank < 2 * lead + 2, picked_a, picked_b)
        corrected = jnp.where(rank == 0, slabs[2], corrected)
        corrected = jnp.where(rank == 1, slabs[3], corrected)
        corrected = jnp.where(rank > part, picked_c, corrected)
        corrected = jnp.where(rank == part, late, corrected)
    return (corrected[None], residual[None])


def solution(mesh):
    in_specs = (
        P("tm", "gz", None, None),
        P("gz", None, None),
        P("gz", None, None),
        P("gz", None, None),
    )
    out_specs = (P("tm", "gz", None, None), P("tm", "gz", None, None))
    return jax.shard_map(shards, mesh=mesh, in_specs=in_specs, out_specs=out_specs, check_vma=False)
```

time: 1310 us -> 326 us (0.25)
  the two profiles are of different devices: /device:TPU:32 before, /device:TPU:57 now
where the time goes in v1:
time: 326 us; the launch traced here: 323 us
  waiting for transfers between devices  163 us (50%)
  Pallas kernels  113 us (35%)
  starting transfers between devices  21 us (6%)
  between operations  14.2 us (4%)
  local copies, waits for them, and re-layouts  8.45 us (3%)
  other arithmetic  3.56 us (1%)
    all_gather x1, waiting for transfers between devices, shards(): own = lax.all_gather(mine, 'tm', axis_index_groups=groups)  101 us
    pallas_call x3, Pallas kernels, run_chain(): pl.pallas_call(functools.partial(chain_kernel, counts, halves), out_shape...  71.8 us
    all_gather x1, waiting for transfers between devices, shards(): gathered = lax.all_gather(fields, 'gz')  45.7 us
    pallas_call x1, Pallas kernels, run_start(): pl.pallas_call(start_kernel, out_shape=[f32(NZ, *PLANE), f32(4, SLAB, *PL...  21.7 us
    pallas_call x1, Pallas kernels, run_fine(): pl.pallas_call(fine_kernel, out_shape=[f32(HALF, *PLANE), f32(HALF, *PLAN...  19.6 us
    ppermute x1, waiting for transfers between devices, shards(): half = lax.ppermute(half, 'tm', pairs)  14.8 us
    slice x2, local copies, waits for them, and re-layouts, shards(): own_a, own_b = (own[:lead], own[lead:])  8.45 us
    ppermute x1, starting transfers between devices, shards(): arrived = lax.ppermute(send, 'tm', swap)  6.65 us
  transfers between devices with their start and end apart: 10, of which 4 were waited for; matrix products, arithmetic and copies ran while one was open for 1% of the time, Pallas kernels for 21%

profile of v1, /device:TPU:57, one launch (start us, length us, event | category | flops | bytes accessed | tf_op | source)
XLA Modules:
  0.0 323.2 jit_solution(9357254551692733006)
XLA Ops:
  7.2 0.0 all-gather.5.cloned.1.call-start
  7.2 1.7 pad_maximum_fusion.1
  8.9 0.0 all-gather.5.cloned.1.call-update
  8.9 0.0 all-gather.7.cloned.1.call-start
  9.0 0.1 pad_add_fusion.3.where
  9.0 45.7 %all-gather.5.cloned.1.call-done = f32[32,4,32,128]{3,2,1,0:T(8,128)} async-done(((f32[4,4,32,128]{3,2,1,0:T(8,128)}), f32[32,4,32,128]{3,2,1,0:T(8,128)}) %all-gather.5.cloned.1.call-update) | async-done | bytes 2097168 | tf_op jit(solution)/shard_map/gather_fields/all_gather | solution.py:393
  54.7 19.6 %fine_spans.1 = (f32[16,32,128]{2,1,0:T(8,128)S(1)}, f32[16,32,128]{2,1,0:T(8,128)S(1)}, f32[4,32,128]{2,1,0:T(8,128)S(1)}, f32[4,32,128]{2,1,0:T(8,128)S(1)}) custom-call(s32[3]{0:T(128)S(1)} %pad_add_fusion.3.where, f32[8,4,4,32,128]{4,3,2,1,0:T(8,128)} %bitcast.43), custom_call_target="tpu_custom_call" | custom-call | flops 42467328 | bytes 94371840 | tf_op jit(solution)/shard_map/fine_spans/pallas_call | solution.py:340
  74.4 6.6 %collective-permute-start = (f32[16,32,128]{2,1,0:T(8,128)S(1)}, f32[16,32,128]{2,1,0:T(8,128)S(1)}, u32[]{:S(2)}, u32[]{:S(2)}) collective-permute-start(f32[16,32,128]{2,1,0:T(8,128)S(1)} %get-tuple-element.16), channel_id=1, source_target_pairs={{0,8},{8,0},{16,24},{24,16},{32,40},{40,32},{48,56},{56,48},{64,72... | collective-permute-start | bytes 786440 | tf_op jit(solution)/shard_map/forcing_halves/ppermute | solution.py:399
  81.0 1.1 collective-permute-done
  82.2 0.9 pad_maximum_fusion
  83.1 0.0 all-gather.7.cloned.1.call-update
  83.1 101.1 %all-gather.7.cloned.1.call-done = f32[32,16,32,128]{3,2,1,0:T(8,128)} async-done(((f32[2,16,32,128]{3,2,1,0:T(8,128)}), f32[32,16,32,128]{3,2,1,0:T(8,128)}) %all-gather.7.cloned.1.call-update) | async-done | bytes 8388624 | tf_op jit(solution)/shard_map/gather_forcing/all_gather | solution.py:403
  184.1 6.6 %slice.28 = f32[24,16,32,128]{3,2,1,0:T(8,128)} slice(f32[32,16,32,128]{3,2,1,0:T(8,128)} %all-gather.7.cloned.1.call-done), slice={[8:32], [0:16], [0:32], [0:128]} | slice | bytes 12582912 | tf_op jit(solution)/shard_map/swap_forcing/slice | solution.py:415
  190.7 2.6 collective-permute-start.2
  193.3 1.9 slice.27
  195.2 1.9 collective-permute-start.1
  197.1 0.1 pad_add_fusion.2.refs_0_
  197.2 0.1 pad_add_fusion.refs_0_
  197.3 21.7 %first_intervals.1 = (f32[32,32,128]{2,1,0:T(8,128)S(1)}, f32[4,4,32,128]{3,2,1,0:T(8,128)S(1)}) custom-call(s32[3]{0:T(128)S(1)} %pad_add_fusion.3.where, f32[8,4,4,32,128]{4,3,2,1,0:T(8,128)} %bitcast.44), custom_call_target="tpu_custom_call" | custom-call | flops 47185920 | bytes 104857600 | tf_op jit(solution)/shard_map/first_intervals/pallas_call | solution.py:352
  219.0 0.0 collective-permute-done.1.refs_4_.refs_5_
  219.0 12.6 %first_chain.2 = (f32[32,32,128]{2,1,0:T(8,128)S(1)}, f32[4,32,128]{2,1,0:T(8,128)S(1)}, f32[4,32,128]{2,1,0:T(8,128)}) custom-call(s32[3]{0:T(128)S(1)} %pad_add_fusion.2.refs_0_, f32[8,4,4,32,128]{4,3,2,1,0:T(8,128)} %bitcast.45, f32[32,32,128]{2,1,0:T(8,128)S(1)} %get-tuple-element.14.refs_2_, f32[4,2,16,32,128]{4,3,2,1,0:T(8,128)} %bitcast.49, ...), custom_call_target="tpu_custom_call" | custom-call | flops 18874368 | bytes 41943040 | tf_op jit(solution)/shard_map/first_chain/pallas_call | solution.py:368
  231.7 0.0 collective-permute-done.2.refs_4_.refs_7_
  231.7 25.8 %first_chain.3 = (f32[16,32,128]{2,1,0:T(8,128)S(1)}, f32[4,32,128]{2,1,0:T(8,128)S(1)}, f32[4,32,128]{2,1,0:T(8,128)S(1)}) custom-call(s32[3]{0:T(128)S(1)} %pad_add_fusion.refs_0_, f32[8,4,4,32,128]{4,3,2,1,0:T(8,128)} %bitcast.46, f32[32,32,128]{2,1,0:T(8,128)S(1)} %get-tuple-element.17.refs_2_, f32[12,2,16,32,128]{4,3,2,1,0:T(8,128)} %bitcast.11.refs_3_.refs_6_, ...), custom_call_target="tpu_custom_call" | custom-call | flops 56623104 | bytes 125829120 | tf_op jit(solution)/shard_map/first_chain/pallas_call | solution.py:368
  257.5 1.3 collective-permute-start.4
  258.8 14.8 %collective-permute-done.4.refs_2_ = f32[16,32,128]{2,1,0:T(8,128)S(1)} collective-permute-done((f32[16,32,128]{2,1,0:T(8,128)S(1)}, f32[16,32,128]{2,1,0:T(8,128)S(1)}, u32[]{:S(2)}, u32[]{:S(2)}) %collective-permute-start.4) | collective-permute-done | bytes 262176 | tf_op jit(solution)/shard_map/hand_over/ppermute | solution.py:433
  273.6 3.2 %collective-permute-start.5 = (f32[16,32,128]{2,1,0:T(8,128)S(1)}, f32[16,32,128]{2,1,0:T(8,128)S(1)}, u32[]{:S(2)}, u32[]{:S(2)}) collective-permute-start(f32[16,32,128]{2,1,0:T(8,128)S(1)} %collective-permute-done.4.refs_2_), channel_id=1, source_target_pairs={{0,8},{8,0},{16,24},{24,16},{32,40},{40,32},{48,56},{56,48},{64,72... | collective-permute-start | bytes 786440 | tf_op jit(solution)/shard_map/hand_over/ppermute | solution.py:434
  276.9 1.9 collective-permute-start.6
  278.8 2.6 collective-permute-start.7
  281.4 0.7 collective-permute-start.3
  282.1 0.1 pad_add_fusion.4.refs_0_
  282.2 33.4 %second_chain.1 = (f32[16,32,128]{2,1,0:T(8,128)}, f32[4,32,128]{2,1,0:T(8,128)S(1)}, f32[4,32,128]{2,1,0:T(8,128)}) custom-call(s32[3]{0:T(128)S(1)} %pad_add_fusion.4.refs_0_, f32[8,4,4,32,128]{4,3,2,1,0:T(8,128)} %bitcast.47, f32[16,32,128]{2,1,0:T(8,128)S(1)} %collective-permute-done.4.refs_2_, f32[16,32,128]{2,1,0:T(8,128)S(1)} %collective-permute-done.5.refs_3_, ...), custom_call_target="tpu_custom_call" | custom-call | flops 75497472 | bytes 167772160 | tf_op jit(solution)/shard_map/second_chain/pallas_call | solution.py:368
  315.6 0.7 fusion.2
  (6 shorter events, 0.0 us)
Async XLA Ops:
  7.2 47.6 %all-gather.5.cloned.1.call-start = ((), (), s32[]{:S(2)}) async-start(), calls=%async_computation | async-start | bytes 2359296 | tf_op jit(solution)/shard_map/gather_fields/all_gather | solution.py:393
  8.9 175.2 %all-gather.7.cloned.1.call-start = ((), (), s32[]{:S(2)}) async-start(), calls=%async_computation.1 | async-start | bytes 8912896 | tf_op jit(solution)/shard_map/gather_forcing/all_gather | solution.py:403
  74.4 7.8 %collective-permute-start = (f32[16,32,128]{2,1,0:T(8,128)S(1)}, f32[16,32,128]{2,1,0:T(8,128)S(1)}, u32[]{:S(2)}, u32[]{:S(2)}) collective-permute-start(f32[16,32,128]{2,1,0:T(8,128)S(1)} %get-tuple-element.16), channel_id=1, source_target_pairs={{0,8},{8,0},{16,24},{24,16},{32,40},{40,32},{48,56},{56,48},{64,72... | collective-permute-start | bytes 786440 | tf_op jit(solution)/shard_map/forcing_halves/ppermute | solution.py:399
  190.7 41.0 %collective-permute-start.2 = (f32[12,2,16,32,128]{4,3,2,1,0:T(8,128)}, f32[12,2,16,32,128]{4,3,2,1,0:T(8,128)}, u32[]{:S(2)}, u32[]{:S(2)}) collective-permute-start(f32[12,2,16,32,128]{4,3,2,1,0:T(8,128)} %bitcast.11.refs_3_.refs_6_), channel_id=1, source_target_pairs={{0,8},{8,0},{16,24},{24,16},{32,40},{40,32},{48,56},{56,48},{64,72... | collective-permute-start | bytes 18874376 | tf_op jit(solution)/shard_map/swap_forcing/ppermute | solution.py:417
  195.2 23.9 %copy-start = (f32[8,16,32,128]{3,2,1,0:T(8,128)}, f32[8,16,32,128]{3,2,1,0:T(8,128)S(1)}, u32[]{:S(2)}) copy-start(f32[8,16,32,128]{3,2,1,0:T(8,128)S(1)} %slice.27) | copy-start | bytes 6291460
  195.2 23.8 %collective-permute-start.1 = (f32[4,2,16,32,128]{4,3,2,1,0:T(8,128)S(1)}, f32[4,2,16,32,128]{4,3,2,1,0:T(8,128)}, u32[]{:S(2)}, u32[]{:S(2)}) collective-permute-start(f32[4,2,16,32,128]{4,3,2,1,0:T(8,128)S(1)} %bitcast.48), channel_id=1, source_target_pairs={{0,8},{8,0},{16,24},{24,16},{32,40},{40,32},{48,56},{56,48},{64,72... | collective-permute-start | bytes 6291464 | tf_op jit(solution)/shard_map/swap_forcing/ppermute | solution.py:416
  257.5 16.1 %collective-permute-start.4 = (f32[16,32,128]{2,1,0:T(8,128)S(1)}, f32[16,32,128]{2,1,0:T(8,128)S(1)}, u32[]{:S(2)}, u32[]{:S(2)}) collective-permute-start(f32[16,32,128]{2,1,0:T(8,128)S(1)} %get-tuple-element.19), channel_id=1, source_target_pairs={{0,448},{8,456},{16,464},{24,472},{32,480},{40,488},{48,496},{56,5... | collective-permute-start | bytes 786440 | tf_op jit(solution)/shard_map/hand_over/ppermute | solution.py:433
  273.6 8.6 %collective-permute-start.5 = (f32[16,32,128]{2,1,0:T(8,128)S(1)}, f32[16,32,128]{2,1,0:T(8,128)S(1)}, u32[]{:S(2)}, u32[]{:S(2)}) collective-permute-start(f32[16,32,128]{2,1,0:T(8,128)S(1)} %collective-permute-done.4.refs_2_), channel_id=1, source_target_pairs={{0,8},{8,0},{16,24},{24,16},{32,40},{40,32},{48,56},{56,48},{64,72... | collective-permute-start | bytes 786440 | tf_op jit(solution)/shard_map/hand_over/ppermute | solution.py:434
  276.9 38.7 %collective-permute-start.6 = (f32[4,32,128]{2,1,0:T(8,128)S(1)}, f32[4,32,128]{2,1,0:T(8,128)S(1)}, u32[]{:S(2)}, u32[]{:S(2)}) collective-permute-start(f32[4,32,128]{2,1,0:T(8,128)S(1)} %get-tuple-element.24), channel_id=1, source_target_pairs={{0,16},{8,24},{16,32},{24,40},{32,48},{40,56},{48,64},{56,72},{64,... | collective-permute-start | bytes 196616 | tf_op jit(solution)/shard_map/residual/ppermute | solution.py:408
  278.8 36.8 %collective-permute-start.7 = (f32[4,32,128]{2,1,0:T(8,128)S(1)}, f32[4,32,128]{2,1,0:T(8,128)S(1)}, u32[]{:S(2)}, u32[]{:S(2)}) collective-permute-start(f32[4,32,128]{2,1,0:T(8,128)S(1)} %get-tuple-element.25), channel_id=1, source_target_pairs={{0,8},{8,16},{16,24},{24,32},{32,40},{40,48},{48,56},{56,64},{64,7... | collective-permute-start | bytes 196616 | tf_op jit(solution)/shard_map/residual/ppermute | solution.py:407
  281.4 34.2 %collective-permute-start.3 = (f32[4,32,128]{2,1,0:T(8,128)S(1)}, f32[4,32,128]{2,1,0:T(8,128)S(1)}, u32[]{:S(2)}, u32[]{:S(2)}) collective-permute-start(f32[4,32,128]{2,1,0:T(8,128)S(1)} %get-tuple-element.18), channel_id=1, source_target_pairs={{192,256},{193,257},{194,258},{195,259},{196,260},{197,261},{198,2... | collective-permute-start | bytes 196616 | tf_op jit(solution)/shard_map/hand_over/ppermute | solution.py:435
Sparse Core Ops, SparseCore 0:
  10.1 44.5 all-gather.4
  83.2 100.8 all-gather.6

commit v2 on v1

v2 whole, which is shorter than its diff:
```python
import functools

import jax
import jax.numpy as jnp
from jax import lax
from jax.experimental import pallas as pl
from jax.experimental.pallas import tpu as pltpu
from jax.sharding import PartitionSpec as P

STEPS = 8
FINE_STEP = 0.01875
COARSE_STEP = FINE_STEP * STEPS
NZ, NX, NY = 32, 32, 128
SLAB = 4
GROUP = 16
ROW = 8
VMEM_BYTES = 48 * 1024 * 1024

PLANE = (NX, NY)
PADDED = (NZ + 2, NX + 16, NY)
MESSAGE = NZ + SLAB


def scratch_set():
    full = pltpu.VMEM((NZ, *PLANE), jnp.float32)
    return [
        pltpu.VMEM(PADDED, jnp.float32),
        pltpu.VMEM(PADDED, jnp.float32),
        pltpu.VMEM((NZ + 1, *PLANE), jnp.float32),
        full,
        full,
        full,
        full,
        full,
        full,
    ]


def put(ref, z, value):
    ref[z + 1, ROW : ROW + NX, :] = value


def get(ref, z):
    return ref[z + 1, ROW : ROW + NX, :]


def clear_edges(ref):
    ref[0] = jnp.zeros(PADDED[1:], jnp.float32)
    ref[NZ + 1] = jnp.zeros(PADDED[1:], jnp.float32)
    for z in range(NZ):
        ref[z + 1, 0:ROW, :] = jnp.zeros((ROW, NY), jnp.float32)
        ref[z + 1, ROW + NX : 2 * ROW + NX, :] = jnp.zeros((ROW, NY), jnp.float32)


def build(a, coefs, kappa, growth, h):
    az, axm, axp, aym, ayp, diag, react = coefs
    half_h = 0.5 * h
    for z in range(NZ):
        put(a, z, kappa(z))
    lane = lax.broadcasted_iota(jnp.int32, PLANE, 1)
    az[0] = half_h * get(a, 0)
    for z in range(NZ):
        k = get(a, z)
        up = half_h * (a[z + 2, ROW : ROW + NX, :] + k)
        down = half_h * (a[z, ROW : ROW + NX, :] + k)
        xm = half_h * (a[z + 1, ROW - 1 : ROW - 1 + NX, :] + k)
        xp = half_h * (a[z + 1, ROW + 1 : ROW + 1 + NX, :] + k)
        ym = half_h * (jnp.where(lane == 0, 0.0, pltpu.roll(k, 1, 1)) + k)
        yp = half_h * (jnp.where(lane == NY - 1, 0.0, pltpu.roll(k, NY - 1, 1)) + k)
        az[z + 1] = up
        axm[z] = xm
        axp[z] = xp
        aym[z] = jnp.where(lane == 0, 0.0, ym)
        ayp[z] = jnp.where(lane == NY - 1, 0.0, yp)
        hr = h * growth(z)
        react[z] = hr
        diag[z] = hr - (up + down + xm + xp + ym + yp)


def step(src, dst, coefs, scale=None, finish=None):
    az, axm, axp, aym, ayp, diag, react = coefs
    below = src[0, ROW : ROW + NX, :]
    here = get(src, 0)
    face = az[0]
    for z in range(NZ):
        above = src[z + 2, ROW : ROW + NX, :]
        next_face = az[z + 1]
        change = here * (diag[z] - react[z] * (here * here))
        change = change + (face * below + next_face * above)
        change = change + (
            axm[z] * src[z + 1, ROW - 1 : ROW - 1 + NX, :]
            + axp[z] * src[z + 1, ROW + 1 : ROW + 1 + NX, :]
        )
        change = change + (aym[z] * pltpu.roll(here, 1, 1) + ayp[z] * pltpu.roll(here, NY - 1, 1))
        if scale is not None:
            change = scale * change
        value = here + change
        if finish is not None:
            value = finish(z, value)
        put(dst, z, value)
        below, here, face = here, above, next_face


def fine(a, b, coefs):
    def pair(i, carry):
        step(a, b, coefs)
        step(b, a, coefs)
        return carry

    lax.fori_loop(0, STEPS // 2, pair, 0)


def copy_slab(src, first, out):
    for i in range(SLAB):
        out[i] = get(src, first + i)


def copy_out(src, out):
    for z in range(NZ):
        out[z] = get(src, z)


def field(gathered, number):
    return lambda z: gathered[z // SLAB, number, z % SLAB]


def fine_kernel(where, gathered, forcing, u_out, w_out, a, b, *coefs):
    first = where[0] * SLAB
    clear_edges(a)
    clear_edges(b)
    build(a, coefs, field(gathered, 1), field(gathered, 2), FINE_STEP)
    for z in range(NZ):
        put(a, z, gathered[z // SLAB, 0, z % SLAB])
    fine(a, b, coefs)
    copy_slab(a, first, u_out)
    step(a, b, coefs, scale=float(STEPS))
    copy_out(b, forcing)
    fine(a, b, coefs)
    copy_slab(a, first, w_out)
    for z in range(NZ):
        forcing[z] = get(a, z) - forcing[z]


def start_kernel(where, gathered, message, slabs, a, b, c, *coefs):
    first = where[0] * SLAB
    clear_edges(a)
    clear_edges(b)
    clear_edges(c)
    build(a, coefs, field(gathered, 1), field(gathered, 2), FINE_STEP)
    for z in range(NZ):
        put(a, z, gathered[z // SLAB, 3, z % SLAB])
    fine(a, b, coefs)
    copy_slab(a, first, slabs.at[0])
    for z in range(NZ):
        put(c, z, get(a, z))
    fine(a, b, coefs)
    copy_slab(a, first, slabs.at[1])
    scale = float(STEPS)
    step(c, b, coefs, scale=scale)
    for z in range(NZ):
        message[z] = get(a, z) - get(b, z)
        put(a, z, gathered[z // SLAB, 3, z % SLAB])
    step(a, b, coefs, scale=scale, finish=lambda z, value: value + (get(c, z) - value))
    for i in range(SLAB):
        message[NZ + i] = get(b, first + i)
    step(b, a, coefs, scale=scale, finish=lambda z, value: value + message[z])
    copy_out(a, message)


def chain_kernel(where, gathered, message, gathered_forcing, message_out, picked, forcing, sems, a, b, *coefs):
    first = where[0] * SLAB
    wanted = where[1]

    def copy_of(index):
        return pltpu.make_async_copy(gathered_forcing.at[index], forcing.at[index], sems.at[index])

    for index in range(GROUP):
        copy_of(index).start()

    clear_edges(a)
    clear_edges(b)
    build(a, coefs, field(gathered, 1), field(gathered, 2), COARSE_STEP)
    for z in range(NZ):
        put(a, z, message[z])

    @pl.when(wanted == 0)
    def _():
        for i in range(SLAB):
            picked[0, i] = message[NZ + i]
            picked[1, i] = get(a, first + i)

    def advance(src, dst, index):
        copy_of(index).wait()
        step(src, dst, coefs, finish=lambda z, value: value + forcing[index, z])

    def pick(src, slot, number):
        for i in range(SLAB):
            picked[slot, i] = get(src, first + i)

    def pair(i, carry):
        advance(a, b, 2 * i)
        advance(b, a, 2 * i + 1)
        number = 2 * i + 2

        @pl.when(number == wanted)
        def _():
            pick(b, 0, number)
            pick(a, 1, number)

        @pl.when(number == wanted + GROUP // 2)
        def _():
            pick(b, 2, number)
            pick(a, 3, number)

        return carry

    lax.fori_loop(0, GROUP // 2, pair, 0)
    copy_out(a, message_out)
    for i in range(SLAB):
        message_out[NZ + i] = get(b, first + i)


def params():
    return pltpu.CompilerParams(vmem_limit_bytes=VMEM_BYTES)


def cost(steps):
    cells = NZ * NX * NY
    return pl.CostEstimate(flops=18 * cells * steps, bytes_accessed=4 * 10 * cells * steps, transcendentals=0)


VMEM_SPEC = pl.BlockSpec(memory_space=pltpu.VMEM)
SMEM_SPEC = pl.BlockSpec(memory_space=pltpu.SMEM)
ANY_SPEC = pl.BlockSpec(memory_space=pl.ANY)


def f32(*shape):
    return jax.ShapeDtypeStruct(shape, jnp.float32)


def run_fine(where, gathered):
    return pl.pallas_call(
        fine_kernel,
        out_shape=[f32(NZ, *PLANE), f32(SLAB, *PLANE), f32(SLAB, *PLANE)],
        in_specs=[SMEM_SPEC, VMEM_SPEC],
        out_specs=[VMEM_SPEC] * 3,
        scratch_shapes=scratch_set(),
        compiler_params=params(),
        cost_estimate=cost(18),
    )(where, gathered)


def run_start(where, gathered):
    return pl.pallas_call(
        start_kernel,
        out_shape=[f32(MESSAGE, *PLANE), f32(2, SLAB, *PLANE)],
        in_specs=[SMEM_SPEC, VMEM_SPEC],
        out_specs=[VMEM_SPEC] * 2,
        scratch_shapes=[pltpu.VMEM(PADDED, jnp.float32)] + scratch_set(),
        compiler_params=params(),
        cost_estimate=cost(20),
    )(where, gathered)


def run_chain(where, gathered, message, forcing):
    return pl.pallas_call(
        chain_kernel,
        out_shape=[f32(MESSAGE, *PLANE), f32(4, SLAB, *PLANE)],
        in_specs=[SMEM_SPEC, VMEM_SPEC, VMEM_SPEC, ANY_SPEC],
        out_specs=[VMEM_SPEC] * 2,
        scratch_shapes=[
            pltpu.VMEM((GROUP, NZ, *PLANE), jnp.float32),
            pltpu.SemaphoreType.DMA((GROUP,)),
        ]
        + scratch_set(),
        compiler_params=params(),
        cost_estimate=cost(GROUP),
    )(where, gathered, message, forcing)


def shards(cpoint_guess, initial_state, diffusivity, growth_rate):
    rank = lax.axis_index("tm")
    z_rank = lax.axis_index("gz")
    count = lax.axis_size("tm")
    groups = count // GROUP
    core = rank % 2
    place = rank % GROUP
    half = GROUP // 2
    where = jnp.stack([z_rank, place]).astype(jnp.int32)

    with jax.named_scope("gather_fields"):
        fields = jnp.stack([cpoint_guess[0], diffusivity, growth_rate, initial_state])
        gathered = lax.all_gather(fields, "gz")
    with jax.named_scope("fine_spans"):
        forcing, u_slab, w_slab = run_fine(where, gathered)
    with jax.named_scope("gather_forcing"):
        members = [[GROUP * g + i for i in range(GROUP)] for g in range(groups)]
        forcing = lax.all_gather(forcing, "tm", axis_index_groups=members)
    with jax.named_scope("first_intervals"):
        message, slabs = run_start(where, gathered)
    with jax.named_scope("residual"):
        u_prev = lax.ppermute(u_slab, "tm", [(i, i + 1) for i in range(count - 1)])
        w_prev = lax.ppermute(w_slab, "tm", [(i, i + 2) for i in range(count - 2)])
        reached = jnp.where(rank == 0, slabs[0], jnp.where(rank == 1, slabs[1], w_prev))
        relaxed = jnp.where(rank == 0, slabs[0], u_prev)
        residual = reached - relaxed
        message, residual = lax.optimization_barrier((message, residual))

    results = None
    for g in range(groups):
        with jax.named_scope("chain"):
            message, picked = run_chain(where, gathered, message, forcing)
        if results is None:
            results = picked
        else:
            results = jnp.where(rank // GROUP == g, picked, results)
        if g + 1 < groups:
            with jax.named_scope("hand_over"):
                hosts = [(GROUP * g + i, GROUP * (g + 1) + i) for i in range(0, half, 2)]
                message = lax.ppermute(message, "tm", hosts)
    with jax.named_scope("spread_results"):
        down = [(i, i + half) for i in range(0, count, 2) if i % GROUP < half]
        pair = lax.ppermute(results[2:], "tm", down)
        pair = jnp.where(place < half, results[:2], pair)
        odd = lax.ppermute(pair[1], "tm", [(i, i + 1) for i in range(0, count, 2)])
        corrected = jnp.where(core == 0, pair[0], odd)
    return (corrected[None], residual[None])


def solution(mesh):
    in_specs = (
        P("tm", "gz", None, None),
        P("gz", None, None),
        P("gz", None, None),
        P("gz", None, None),
    )
    out_specs = (P("tm", "gz", None, None), P("tm", "gz", None, None))
    return jax.shard_map(shards, mesh=mesh, in_specs=in_specs, out_specs=out_specs, check_vma=False)
```

time: 326 us -> 210 us (0.64)
  Pallas kernels: 113 us -> 49.2 us
  waiting for transfers between devices: 163 us -> 122 us
  starting transfers between devices: 21 us -> 15.4 us
  local copies, waits for them, and re-layouts: 8.45 us -> 4.79 us
    pallas_call x5 -> x6, Pallas kernels: 113 us -> 49.2 us  [the longest x4 33.4 us: run_chain(): pl.pallas_call(chain_kernel, out_shape=[f32(MESSAGE, *PLANE), f32(4, SLAB...]
    all_gather x1, waiting for transfers between devices: 101 us -> 38.8 us  [shards(): forcing = lax.all_gather(forcing, 'tm', axis_index_groups=members)]
    ppermute x6 -> x5, waiting for transfers between devices: 15.9 us -> 37.8 us  [the longest x1 37.8 us: shards(): odd = lax.ppermute(pair[1], 'tm', [(i, i + 1) for i in range(0, count, 2)])]
    ppermute x6 -> x5, starting transfers between devices: 16.3 us -> 4.19 us  [the longest x3 2.23 us: shards(): message = lax.ppermute(message, 'tm', hosts)]
    slice x2 -> x1, local copies, waits for them, and re-layouts: 8.45 us -> 0.01 us  [shards(): pair = lax.ppermute(results[2:], 'tm', down)]
    ppermute x1, starting transfers between devices: 2.64 us -> 8 us  [shards(): u_prev = lax.ppermute(u_slab, 'tm', [(i, i + 1) for i in range(count - 1)])]
    unnamed x2 -> x8, local copies, waits for them, and re-layouts: 0.01 us -> 4.77 us
  transfers between devices with their start and end apart: 10 -> 9, of which waited for: 4 -> 3; matrix products, arithmetic and copies ran while one was open for 1% -> 0% of each run, Pallas kernels for 21% -> 4%
where the time goes in v2:
time: 210 us; the launch traced here: 209 us
  waiting for transfers between devices  122 us (58%)
  Pallas kernels  49.2 us (23%)
  starting transfers between devices  15.4 us (7%)
  between operations  14.3 us (7%)
  local copies, waits for them, and re-layouts  4.79 us (2%)
  other arithmetic  3.13 us (1%)
    all_gather x1, waiting for transfers between devices, shards(): gathered = lax.all_gather(fields, 'gz')  45.7 us
    all_gather x1, waiting for transfers between devices, shards(): forcing = lax.all_gather(forcing, 'tm', axis_index_groups=members)  38.8 us
    ppermute x1, waiting for transfers between devices, shards(): odd = lax.ppermute(pair[1], 'tm', [(i, i + 1) for i in range(0, count, 2)])  37.8 us
    pallas_call x4, Pallas kernels, run_chain(): pl.pallas_call(chain_kernel, out_shape=[f32(MESSAGE, *PLANE), f32(4, SLAB...  33.4 us
    ppermute x1, starting transfers between devices, shards(): u_prev = lax.ppermute(u_slab, 'tm', [(i, i + 1) for i in range(count - 1)])  8 us
    pallas_call x1, Pallas kernels, run_start(): pl.pallas_call(start_kernel, out_shape=[f32(MESSAGE, *PLANE), f32(2, SLAB...  7.92 us
    pallas_call x1, Pallas kernels, run_fine(): pl.pallas_call(fine_kernel, out_shape=[f32(NZ, *PLANE), f32(SLAB, *PLANE)...  7.88 us
    unnamed x8, local copies, waits for them, and re-layouts  4.77 us
  transfers between devices with their start and end apart: 9, of which 3 were waited for; matrix products, arithmetic and copies ran while one was open for 0% of the time, Pallas kernels for 4%

profile of v2, /device:TPU:57, one launch (start us, length us, event | category | flops | bytes accessed | tf_op | source)
XLA Modules:
  0.0 209.1 jit_solution(6145663431122759244)
XLA Ops:
  7.2 0.0 all-gather.5.cloned.1.call-start
  7.2 1.7 pad_maximum_fusion
  8.9 0.0 all-gather.5.cloned.1.call-update
  8.9 0.0 all-gather.7.cloned.1.call-start
  9.0 0.1 pad_add_fusion.where
  9.0 45.7 %all-gather.5.cloned.1.call-done = f32[32,4,32,128]{3,2,1,0:T(8,128)} async-done(((f32[4,4,32,128]{3,2,1,0:T(8,128)}), f32[32,4,32,128]{3,2,1,0:T(8,128)}) %all-gather.5.cloned.1.call-update) | async-done | bytes 2097168 | tf_op jit(solution)/shard_map/gather_fields/all_gather | solution.py:293
  54.7 1.6 copy-done
  56.3 7.9 %fine_spans.1 = (f32[32,32,128]{2,1,0:T(8,128)}, f32[4,32,128]{2,1,0:T(8,128)S(1)}, f32[4,32,128]{2,1,0:T(8,128)S(1)}) custom-call(s32[2]{0:T(128)S(1)} %pad_add_fusion.where, f32[8,4,4,32,128]{4,3,2,1,0:T(8,128)S(1)} %bitcast.29), custom_call_target="tpu_custom_call" | custom-call | flops 42467328 | bytes 94371840 | tf_op jit(solution)/shard_map/fine_spans/pallas_call | solution.py:242
  64.2 0.0 all-gather.7.cloned.1.call-update
  64.2 3.1 %collective-permute-start = (f32[4,32,128]{2,1,0:T(8,128)S(1)}, f32[4,32,128]{2,1,0:T(8,128)S(1)}, u32[]{:S(2)}, u32[]{:S(2)}) collective-permute-start(f32[4,32,128]{2,1,0:T(8,128)S(1)} %get-tuple-element.18), channel_id=1, source_target_pairs={{0,16},{8,24},{16,32},{24,40},{32,48},{40,56},{48,64},{56,72},{64,... | collective-permute-start | bytes 196616 | tf_op jit(solution)/shard_map/residual/ppermute | solution.py:303
  67.3 8.0 %collective-permute-start.1 = (f32[4,32,128]{2,1,0:T(8,128)S(1)}, f32[4,32,128]{2,1,0:T(8,128)S(1)}, u32[]{:S(2)}, u32[]{:S(2)}) collective-permute-start(f32[4,32,128]{2,1,0:T(8,128)S(1)} %get-tuple-element.19), channel_id=1, source_target_pairs={{0,8},{8,16},{16,24},{24,32},{32,40},{40,48},{48,56},{56,64},{64,7... | collective-permute-start | bytes 196616 | tf_op jit(solution)/shard_map/residual/ppermute | solution.py:302
  75.3 1.6 copy-done.1
  76.9 7.9 %first_intervals.1 = (f32[36,32,128]{2,1,0:T(8,128)S(1)}, f32[2,4,32,128]{3,2,1,0:T(8,128)S(1)}) custom-call(s32[2]{0:T(128)S(1)} %pad_add_fusion.where, f32[8,4,4,32,128]{4,3,2,1,0:T(8,128)S(1)} %bitcast.30), custom_call_target="tpu_custom_call" | custom-call | flops 47185920 | bytes 104857600 | tf_op jit(solution)/shard_map/first_intervals/pallas_call | solution.py:254
  84.9 0.0 collective-permute-done
  84.9 0.7 fusion.3
  85.5 38.8 %all-gather.7.cloned.1.call-done = f32[512,32,128]{2,1,0:T(8,128)} async-done(((f32[32,32,128]{2,1,0:T(8,128)}), f32[512,32,128]{2,1,0:T(8,128)}) %all-gather.7.cloned.1.call-update) | async-done | bytes 8388624 | tf_op jit(solution)/shard_map/gather_forcing/all_gather | solution.py:298
  124.4 1.6 copy-done.2
  125.9 7.9 %chain.4 = (f32[36,32,128]{2,1,0:T(8,128)S(1)}, f32[4,4,32,128]{3,2,1,0:T(8,128)S(1)}) custom-call(s32[2]{0:T(128)S(1)} %pad_add_fusion.where, f32[8,4,4,32,128]{4,3,2,1,0:T(8,128)S(1)} %bitcast.31, f32[36,32,128]{2,1,0:T(8,128)S(1)} %get-tuple-element.20.message, f32[16,32,32,128]{3,2,1,0:T(8,128)} %bitcast.35), custom_call_target="tpu_custom_call" | custom-call | flops 37748736 | bytes 83886080 | tf_op jit(solution)/shard_map/chain/pallas_call | solution.py:266
  133.9 0.8 collective-permute-start.2
  134.7 0.0 collective-permute-done.2.message
  134.7 7.9 %chain.5 = (f32[36,32,128]{2,1,0:T(8,128)S(1)}, f32[4,4,32,128]{3,2,1,0:T(8,128)S(1)}) custom-call(s32[2]{0:T(128)S(1)} %pad_add_fusion.where, f32[8,4,4,32,128]{4,3,2,1,0:T(8,128)S(1)} %bitcast.32, f32[36,32,128]{2,1,0:T(8,128)S(1)} %collective-permute-done.2.message, f32[16,32,32,128]{3,2,1,0:T(8,128)} %bitcast.36), custom_call_target="tpu_custom_call" | custom-call | flops 37748736 | bytes 83886080 | tf_op jit(solution)/shard_map/chain/pallas_call | solution.py:266
  142.7 0.7 collective-permute-start.3
  143.4 0.0 collective-permute-done.3.message
  143.4 8.8 %chain.6 = (f32[36,32,128]{2,1,0:T(8,128)}, f32[4,4,32,128]{3,2,1,0:T(8,128)S(1)}) custom-call(s32[2]{0:T(128)S(1)} %pad_add_fusion.where, f32[8,4,4,32,128]{4,3,2,1,0:T(8,128)S(1)} %bitcast.33, f32[36,32,128]{2,1,0:T(8,128)S(1)} %collective-permute-done.3.message, f32[16,32,32,128]{3,2,1,0:T(8,128)} %bitcast.37), custom_call_target="tpu_custom_call" | custom-call | flops 37748736 | bytes 83886080 | tf_op jit(solution)/shard_map/chain/pallas_call | solution.py:266
  152.1 0.7 collective-permute-start.4
  152.9 0.0 collective-permute-done.4.message
  152.9 8.8 %chain.7 = (f32[36,32,128]{2,1,0:T(8,128)}, f32[4,4,32,128]{3,2,1,0:T(8,128)S(1)}) custom-call(s32[2]{0:T(128)S(1)} %pad_add_fusion.where, f32[8,4,4,32,128]{4,3,2,1,0:T(8,128)S(1)} %bitcast.34, f32[36,32,128]{2,1,0:T(8,128)S(1)} %collective-permute-done.4.message, f32[16,32,32,128]{3,2,1,0:T(8,128)} %bitcast.38), custom_call_target="tpu_custom_call" | custom-call | flops 37748736 | bytes 83886080 | tf_op jit(solution)/shard_map/chain/pallas_call | solution.py:266
  161.7 0.1 select_select_fusion
  161.8 0.7 collective-permute-start.5
  162.5 1.3 collective-permute-start.6
  163.8 37.8 %collective-permute-done.6 = f32[4,32,128]{2,1,0:T(8,128)S(1)} collective-permute-done((f32[4,32,128]{2,1,0:T(8,128)S(1)}, f32[4,32,128]{2,1,0:T(8,128)S(1)}, u32[]{:S(2)}, u32[]{:S(2)}) %collective-permute-start.6) | collective-permute-done | bytes 65568 | tf_op jit(solution)/shard_map/spread_results/ppermute | solution.py:325
  201.6 0.6 fusion.1
  (10 shorter events, 0.1 us)
Async XLA Ops:
  7.2 47.6 %all-gather.5.cloned.1.call-start = ((), (), s32[]{:S(2)}) async-start(), calls=%async_computation | async-start | bytes 2359296 | tf_op jit(solution)/shard_map/gather_fields/all_gather | solution.py:293
  8.9 115.5 %all-gather.7.cloned.1.call-start = ((), (), s32[]{:S(2)}) async-start(), calls=%async_computation.1 | async-start | bytes 8912896 | tf_op jit(solution)/shard_map/gather_forcing/all_gather | solution.py:298
  54.7 1.6 copy-start
  64.2 20.6 %collective-permute-start = (f32[4,32,128]{2,1,0:T(8,128)S(1)}, f32[4,32,128]{2,1,0:T(8,128)S(1)}, u32[]{:S(2)}, u32[]{:S(2)}) collective-permute-start(f32[4,32,128]{2,1,0:T(8,128)S(1)} %get-tuple-element.18), channel_id=1, source_target_pairs={{0,16},{8,24},{16,32},{24,40},{32,48},{40,56},{48,64},{56,72},{64,... | collective-permute-start | bytes 196616 | tf_op jit(solution)/shard_map/residual/ppermute | solution.py:303
  67.3 17.6 %collective-permute-start.1 = (f32[4,32,128]{2,1,0:T(8,128)S(1)}, f32[4,32,128]{2,1,0:T(8,128)S(1)}, u32[]{:S(2)}, u32[]{:S(2)}) collective-permute-start(f32[4,32,128]{2,1,0:T(8,128)S(1)} %get-tuple-element.19), channel_id=1, source_target_pairs={{0,8},{8,16},{16,24},{24,32},{32,40},{40,48},{48,56},{56,64},{64,7... | collective-permute-start | bytes 196616 | tf_op jit(solution)/shard_map/residual/ppermute | solution.py:302
  75.3 1.6 copy-start.1
  124.4 1.6 copy-start.2
  133.9 19.0 %copy-start.3 = (f32[32,4,32,128]{3,2,1,0:T(8,128)S(1)}, f32[32,4,32,128]{3,2,1,0:T(8,128)}, u32[]{:S(2)}) copy-start(f32[32,4,32,128]{3,2,1,0:T(8,128)} %all-gather.5.cloned.1.call-done) | copy-start | bytes 6291460
  133.9 0.8 collective-permute-start.2
  142.7 0.7 collective-permute-start.3
  152.1 0.7 collective-permute-start.4
  161.8 0.7 collective-permute-start.5
  162.5 39.1 %collective-permute-start.6 = (f32[4,32,128]{2,1,0:T(8,128)S(1)}, f32[4,32,128]{2,1,0:T(8,128)S(1)}, u32[]{:S(2)}, u32[]{:S(2)}) collective-permute-start(f32[4,32,128]{2,1,0:T(8,128)S(1)} %slice_bitcast_fusion), channel_id=1, source_target_pairs={{0,8},{16,24},{32,40},{48,56},{64,72},{80,88},{96,104},{112,120},{... | collective-permute-start | bytes 196616 | tf_op jit(solution)/shard_map/spread_results/ppermute | solution.py:325
Sparse Core Ops, SparseCore 0:
  10.1 44.5 all-gather.4
  64.3 59.9 all-gather.6

commit v3 on v2

--- a/solution.py
+++ b/solution.py
@@ -12,28 +12,19 @@
 COARSE_STEP = FINE_STEP * STEPS
 NZ, NX, NY = 32, 32, 128
 SLAB = 4
+SHARE = 2
 GROUP = 16
 ROW = 8
 VMEM_BYTES = 48 * 1024 * 1024
 
 PLANE = (NX, NY)
 PADDED = (NZ + 2, NX + 16, NY)
+COEFFICIENTS = [(NZ + 1, *PLANE)] + [(NZ, *PLANE)] * 5
 MESSAGE = NZ + SLAB
 
 
 def scratch_set():
-    full = pltpu.VMEM((NZ, *PLANE), jnp.float32)
-    return [
-        pltpu.VMEM(PADDED, jnp.float32),
-        pltpu.VMEM(PADDED, jnp.float32),
-        pltpu.VMEM((NZ + 1, *PLANE), jnp.float32),
-        full,
-        full,
-        full,
-        full,
-        full,
-        full,
-    ]
+    return [pltpu.VMEM(PADDED, jnp.float32)] * 2 + [pltpu.VMEM(shape, jnp.float32) for shape in COEFFICIENTS]
 
 
 def put(ref, z, value):
@@ -53,48 +44,46 @@
 
 
 def build(a, coefs, kappa, growth, h):
-    az, axm, axp, aym, ayp, diag, react = coefs
+    az, ax, aym, ayp, diag, react = coefs
     half_h = 0.5 * h
     for z in range(NZ):
         put(a, z, kappa(z))
+    row = lax.broadcasted_iota(jnp.int32, PLANE, 0)
     lane = lax.broadcasted_iota(jnp.int32, PLANE, 1)
     az[0] = half_h * get(a, 0)
     for z in range(NZ):
         k = get(a, z)
         up = half_h * (a[z + 2, ROW : ROW + NX, :] + k)
         down = half_h * (a[z, ROW : ROW + NX, :] + k)
-        xm = half_h * (a[z + 1, ROW - 1 : ROW - 1 + NX, :] + k)
-        xp = half_h * (a[z + 1, ROW + 1 : ROW + 1 + NX, :] + k)
         ym = half_h * (jnp.where(lane == 0, 0.0, pltpu.roll(k, 1, 1)) + k)
         yp = half_h * (jnp.where(lane == NY - 1, 0.0, pltpu.roll(k, NY - 1, 1)) + k)
+        ends = jnp.where((row == 0) | (row == NX - 1), half_h * k, 0.0)
+        xp = half_h * (a[z + 1, ROW + 1 : ROW + 1 + NX, :] + k)
         az[z + 1] = up
-        axm[z] = xm
-        axp[z] = xp
+        ax[z] = jnp.where(row == NX - 1, 0.0, xp)
         aym[z] = jnp.where(lane == 0, 0.0, ym)
         ayp[z] = jnp.where(lane == NY - 1, 0.0, yp)
         hr = h * growth(z)
         react[z] = hr
-        diag[z] = hr - (up + down + xm + xp + ym + yp)
+        diag[z] = 1.0 + (hr - (up + down + ends + ym + yp))
 
 
 def step(src, dst, coefs, scale=None, finish=None):
-    az, axm, axp, aym, ayp, diag, react = coefs
+    az, ax, aym, ayp, diag, react = coefs
     below = src[0, ROW : ROW + NX, :]
     here = get(src, 0)
     face = az[0]
     for z in range(NZ):
         above = src[z + 2, ROW : ROW + NX, :]
         next_face = az[z + 1]
-        change = here * (diag[z] - react[z] * (here * here))
-        change = change + (face * below + next_face * above)
-        change = change + (
-            axm[z] * src[z + 1, ROW - 1 : ROW - 1 + NX, :]
-            + axp[z] * src[z + 1, ROW + 1 : ROW + 1 + NX, :]
-        )
-        change = change + (aym[z] * pltpu.roll(here, 1, 1) + ayp[z] * pltpu.roll(here, NY - 1, 1))
+        centre = diag[z] if scale is None else diag[z] - 1.0
+        value = here * (centre - react[z] * (here * here))
+        value = value + (face * below + next_face * above)
+        flux = ax[z] * (src[z + 1, ROW + 1 : ROW + 1 + NX, :] - here)
+        value = value + (flux - pltpu.roll(flux, 1, 0))
+        value = value + (aym[z] * pltpu.roll(here, 1, 1) + ayp[z] * pltpu.roll(here, NY - 1, 1))
         if scale is not None:
-            change = scale * change
-        value = here + change
+            value = here + scale * value
         if finish is not None:
             value = finish(z, value)
         put(dst, z, value)
@@ -120,17 +109,27 @@
         out[z] = get(src, z)
 
 
-def field(gathered, number):
-    return lambda z: gathered[z // SLAB, number, z % SLAB]
-
-
-def fine_kernel(where, gathered, forcing, u_out, w_out, a, b, *coefs):
+def kappa_of(fields):
+    return lambda z: fields[z % SLAB, z // SLAB]
+
+
+def growth_of(fields):
+    return lambda z: fields[SLAB + z % SLAB, z // SLAB]
+
+
+def fine_kernel(where, gathered, piece1, piece2, piece3, forcing, u_out, w_out, fields, a, b, *coefs):
     first = where[0] * SLAB
+    quarter = where[2]
+    for slab in range(NZ // SLAB):
+        for i in range(SHARE):
+            fields[SHARE * quarter + i, slab] = gathered[slab, SLAB + i]
+            for j, piece in enumerate((piece1, piece2, piece3)):
+                fields[SHARE * (quarter ^ (j + 1)) + i, slab] = piece[slab, i]
     clear_edges(a)
     clear_edges(b)
-    build(a, coefs, field(gathered, 1), field(gathered, 2), FINE_STEP)
-    for z in range(NZ):
-        put(a, z, gathered[z // SLAB, 0, z % SLAB])
+    build(a, coefs, kappa_of(fields), growth_of(fields), FINE_STEP)
+    for z in range(NZ):
+        put(a, z, gathered[z // SLAB, z % SLAB])
     fine(a, b, coefs)
     copy_slab(a, first, u_out)
     step(a, b, coefs, scale=float(STEPS))
@@ -141,14 +140,14 @@
         forcing[z] = get(a, z) - forcing[z]
 
 
-def start_kernel(where, gathered, message, slabs, a, b, c, *coefs):
+def start_kernel(where, fields, initial, message, slabs, a, b, c, *coefs):
     first = where[0] * SLAB
     clear_edges(a)
     clear_edges(b)
     clear_edges(c)
-    build(a, coefs, field(gathered, 1), field(gathered, 2), FINE_STEP)
-    for z in range(NZ):
-        put(a, z, gathered[z // SLAB, 3, z % SLAB])
+    build(a, coefs, kappa_of(fields), growth_of(fields), FINE_STEP)
+    for z in range(NZ):
+        put(a, z, initial[z // SLAB, z % SLAB])
     fine(a, b, coefs)
     copy_slab(a, first, slabs.at[0])
     for z in range(NZ):
@@ -159,7 +158,7 @@
     step(c, b, coefs, scale=scale)
     for z in range(NZ):
         message[z] = get(a, z) - get(b, z)
-        put(a, z, gathered[z // SLAB, 3, z % SLAB])
+        put(a, z, initial[z // SLAB, z % SLAB])
     step(a, b, coefs, scale=scale, finish=lambda z, value: value + (get(c, z) - value))
     for i in range(SLAB):
         message[NZ + i] = get(b, first + i)
@@ -167,7 +166,11 @@
     copy_out(a, message)
 
 
-def chain_kernel(where, gathered, message, gathered_forcing, message_out, picked, forcing, sems, a, b, *coefs):
+def chain_kernel(last, where, fields, message, gathered_forcing, *refs):
+    if last:
+        picked, forcing, sems, a, b, *coefs = refs
+    else:
+        message_out, picked, forcing, sems, a, b, *coefs = refs
     first = where[0] * SLAB
     wanted = where[1]
 
@@ -179,7 +182,7 @@
 
     clear_edges(a)
     clear_edges(b)
-    build(a, coefs, field(gathered, 1), field(gathered, 2), COARSE_STEP)
+    build(a, coefs, kappa_of(fields), growth_of(fields), COARSE_STEP)
     for z in range(NZ):
         put(a, z, message[z])
 
@@ -215,9 +218,10 @@
         return carry
 
     lax.fori_loop(0, GROUP // 2, pair, 0)
-    copy_out(a, message_out)
-    for i in range(SLAB):
-        message_out[NZ + i] = get(b, first + i)
+    if not last:
+        copy_out(a, message_out)
+        for i in range(SLAB):
+            message_out[NZ + i] = get(b, first + i)
 
 
 def params():
@@ -238,36 +242,42 @@
     return jax.ShapeDtypeStruct(shape, jnp.float32)
 
 
-def run_fine(where, gathered):
+def run_fine(where, gathered, pieces):
     return pl.pallas_call(
         fine_kernel,
-        out_shape=[f32(NZ, *PLANE), f32(SLAB, *PLANE), f32(SLAB, *PLANE)],
-        in_specs=[SMEM_SPEC, VMEM_SPEC],
-        out_specs=[VMEM_SPEC] * 3,
+        out_shape=[
+            f32(NZ, *PLANE),
+            f32(SLAB, *PLANE),
+            f32(SLAB, *PLANE),
+            f32(2 * SLAB, NZ // SLAB, *PLANE),
+        ],
+        in_specs=[SMEM_SPEC] + [VMEM_SPEC] * 4,
+        out_specs=[VMEM_SPEC] * 4,
         scratch_shapes=scratch_set(),
         compiler_params=params(),
         cost_estimate=cost(18),
-    )(where, gathered)
-
-
-def run_start(where, gathered):
+    )(where, gathered, *pieces)
+
+
+def run_start(where, fields, initial):
     return pl.pallas_call(
         start_kernel,
         out_shape=[f32(MESSAGE, *PLANE), f32(2, SLAB, *PLANE)],
-        in_specs=[SMEM_SPEC, VMEM_SPEC],
+        in_specs=[SMEM_SPEC, VMEM_SPEC, VMEM_SPEC],
         out_specs=[VMEM_SPEC] * 2,
         scratch_shapes=[pltpu.VMEM(PADDED, jnp.float32)] + scratch_set(),
         compiler_params=params(),
         cost_estimate=cost(20),
-    )(where, gathered)
-
-
-def run_chain(where, gathered, message, forcing):
+    )(where, fields, initial)
+
+
+def run_chain(where, fields, message, forcing, last):
+    outs = ([] if last else [f32(MESSAGE, *PLANE)]) + [f32(4, SLAB, *PLANE)]
     return pl.pallas_call(
-        chain_kernel,
-        out_shape=[f32(MESSAGE, *PLANE), f32(4, SLAB, *PLANE)],
+        functools.partial(chain_kernel, last),
+        out_shape=outs,
         in_specs=[SMEM_SPEC, VMEM_SPEC, VMEM_SPEC, ANY_SPEC],
-        out_specs=[VMEM_SPEC] * 2,
+        out_specs=[VMEM_SPEC] * len(outs),
         scratch_shapes=[
             pltpu.VMEM((GROUP, NZ, *PLANE), jnp.float32),
             pltpu.SemaphoreType.DMA((GROUP,)),
@@ -275,7 +285,7 @@
         + scratch_set(),
         compiler_params=params(),
         cost_estimate=cost(GROUP),
-    )(where, gathered, message, forcing)
+    )(where, fields, message, forcing)
 
 
 def shards(cpoint_guess, initial_state, diffusivity, growth_rate):
@@ -286,18 +296,30 @@
     core = rank % 2
     place = rank % GROUP
     half = GROUP // 2
-    where = jnp.stack([z_rank, place]).astype(jnp.int32)
+    quarter = rank % 4
+    where = jnp.stack([z_rank, place, quarter]).astype(jnp.int32)
+    across = [(i, i ^ 2) for i in range(count)]
+    swap = [(i, i ^ 1) for i in range(count)]
 
     with jax.named_scope("gather_fields"):
-        fields = jnp.stack([cpoint_guess[0], diffusivity, growth_rate, initial_state])
-        gathered = lax.all_gather(fields, "gz")
+        low = jnp.where(quarter % 2 == 0, diffusivity[:SHARE], diffusivity[SHARE:])
+        high = jnp.where(quarter % 2 == 0, growth_rate[:SHARE], growth_rate[SHARE:])
+        share = jnp.where(quarter < 2, low, high)
+        gathered = lax.all_gather(jnp.concatenate([cpoint_guess[0], share]), "gz")
+    with jax.named_scope("share_coefficients"):
+        share = gathered[:, SLAB:]
+        piece2 = lax.ppermute(share, "tm", across)
+        piece1 = lax.ppermute(share, "tm", swap)
+        piece3 = lax.ppermute(piece2, "tm", swap)
     with jax.named_scope("fine_spans"):
-        forcing, u_slab, w_slab = run_fine(where, gathered)
+        forcing, u_slab, w_slab, fields = run_fine(where, gathered, (piece1, piece2, piece3))
     with jax.named_scope("gather_forcing"):
         members = [[GROUP * g + i for i in range(GROUP)] for g in range(groups)]
         forcing = lax.all_gather(forcing, "tm", axis_index_groups=members)
     with jax.named_scope("first_intervals"):
-        message, slabs = run_start(where, gathered)
+        initial, u_slab = lax.optimization_barrier((initial_state, u_slab))
+        initial = lax.all_gather(initial, "gz")
+        message, slabs = run_start(where, fields, initial)
     with jax.named_scope("residual"):
         u_prev = lax.ppermute(u_slab, "tm", [(i, i + 1) for i in range(count - 1)])
         w_prev = lax.ppermute(w_slab, "tm", [(i, i + 2) for i in range(count - 2)])
@@ -309,7 +331,7 @@
     results = None
     for g in range(groups):
         with jax.named_scope("chain"):
-            message, picked = run_chain(where, gathered, message, forcing)
+            *message, picked = run_chain(where, fields, message, forcing, g + 1 == groups)
         if results is None:
             results = picked
         else:
@@ -317,7 +339,7 @@
         if g + 1 < groups:
             with jax.named_scope("hand_over"):
                 hosts = [(GROUP * g + i, GROUP * (g + 1) + i) for i in range(0, half, 2)]
-                message = lax.ppermute(message, "tm", hosts)
+                message = lax.ppermute(message[0], "tm", hosts)
     with jax.named_scope("spread_results"):
         down = [(i, i + half) for i in range(0, count, 2) if i % GROUP < half]
         pair = lax.ppermute(results[2:], "tm", down)

time: 210 us -> 196 us (0.933)
  waiting for transfers between devices: 122 us -> 59 us
  blocking collectives: 0 us -> 47.7 us
  starting transfers between devices: 15.4 us -> 26.6 us
  local copies, waits for them, and re-layouts: 4.79 us -> 0.03 us
  Pallas kernels: 49.2 us -> 45.1 us
    all_gather x0 -> x2, blocking collectives: none -> 47.7 us  [the longest x1 27.3 us: shards(): gathered = lax.all_gather(jnp.concatenate([cpoint_guess[0], share]), 'gz')]
    all_gather x1 -> x0, waiting for transfers between devices: 45.7 us -> none  [shards(): gathered = lax.all_gather(fields, 'gz')]
    all_gather x1, waiting for transfers between devices: 38.8 us -> 20.3 us  [shards(): forcing = lax.all_gather(forcing, 'tm', axis_index_groups=members)]
    ppermute x3 -> x6, starting transfers between devices: 2.23 us -> 18.1 us  [the longest x1 8.09 us: shards(): piece1 = lax.ppermute(share, 'tm', swap)]
    unnamed x8 -> x0, local copies, waits for them, and re-layouts: 4.77 us -> none
    ppermute x1, starting transfers between devices: 8 us -> 3.38 us  [shards(): u_prev = lax.ppermute(u_slab, 'tm', [(i, i + 1) for i in range(count - 1)])]
    pallas_call x4, Pallas kernels: 33.4 us -> 30 us  [run_chain(): pl.pallas_call(functools.partial(chain_kernel, last), out_shape=outs, in_...]
  transfers between devices with their start and end apart: 9 -> 11, of which waited for: 3 -> 3; matrix products, arithmetic and copies ran while one was open for 0% -> 0% of each run, Pallas kernels for 4% -> 4%
where the time goes in v3:
time: 196 us
  waiting for transfers between devices  59 us (30%)
  blocking collectives  47.7 us (24%)
  Pallas kernels  45.1 us (23%)
  starting transfers between devices  26.6 us (14%)
  between operations  14.3 us (7%)
  other arithmetic  3.16 us (2%)
    ppermute x1, waiting for transfers between devices, shards(): odd = lax.ppermute(pair[1], 'tm', [(i, i + 1) for i in range(0, count, 2)])  37.6 us
    pallas_call x4, Pallas kernels, run_chain(): pl.pallas_call(functools.partial(chain_kernel, last), out_shape=outs, in_...  30 us
    all_gather x1, blocking collectives, shards(): gathered = lax.all_gather(jnp.concatenate([cpoint_guess[0], share]), 'gz')  27.3 us
    all_gather x1, blocking collectives, shards(): initial = lax.all_gather(initial, 'gz')  20.4 us
    all_gather x1, waiting for transfers between devices, shards(): forcing = lax.all_gather(forcing, 'tm', axis_index_groups=members)  20.3 us
    ppermute x1, starting transfers between devices, shards(): piece1 = lax.ppermute(share, 'tm', swap)  8.09 us
    pallas_call x1, Pallas kernels, run_fine(): pl.pallas_call(fine_kernel, out_shape=[f32(NZ, *PLANE), f32(SLAB, *PLANE)...  7.54 us
    pallas_call x1, Pallas kernels, run_start(): pl.pallas_call(start_kernel, out_shape=[f32(MESSAGE, *PLANE), f32(2, SLAB...  7.5 us
  transfers between devices with their start and end apart: 11, of which 3 were waited for; matrix products, arithmetic and copies ran while one was open for 0% of the time, Pallas kernels for 4%

profile of v3, /device:TPU:57, one launch (start us, length us, event | category | flops | bytes accessed | tf_op | source)
XLA Modules:
  0.0 195.8 jit_solution(17358451171160805258)
XLA Ops:
  7.2 0.0 all-gather.5.cloned.1.call-start
  7.2 0.8 select_select_fusion.1
  8.1 0.8 pad_maximum_fusion
  8.9 27.3 %all-gather = f32[48,32,128]{2,1,0:T(8,128)S(1)} all-gather(f32[6,32,128]{2,1,0:T(8,128)S(1)} %pad_maximum_fusion), channel_id=2, replica_groups=mesh['tm'=64,'gz'=8] {'gz'}, dimensions={0}, use_global_device_ids=true | all-gather | bytes 884736 | tf_op jit(solution)/shard_map/gather_fields/all_gather | solution.py:308
  36.2 3.1 %collective-permute-start.1 = (f32[8,2,32,128]{3,2,1,0:T(8,128)S(1)}, f32[8,2,32,128]{3,2,1,0:T(8,128)S(1)}, u32[]{:S(2)}, u32[]{:S(2)}) collective-permute-start(f32[8,2,32,128]{3,2,1,0:T(8,128)S(1)} %slice.45), channel_id=1, source_target_pairs={{0,16},{8,24},{16,0},{24,8},{32,48},{40,56},{48,32},{56,40},{64,80... | collective-permute-start | bytes 786440 | tf_op jit(solution)/shard_map/share_coefficients/ppermute | solution.py:311
  39.3 8.1 %collective-permute-start = (f32[8,2,32,128]{3,2,1,0:T(8,128)S(1)}, f32[8,2,32,128]{3,2,1,0:T(8,128)S(1)}, u32[]{:S(2)}, u32[]{:S(2)}) collective-permute-start(f32[8,2,32,128]{3,2,1,0:T(8,128)S(1)} %slice.45), channel_id=1, source_target_pairs={{0,8},{8,0},{16,24},{24,16},{32,40},{40,32},{48,56},{56,48},{64,72... | collective-permute-start | bytes 786440 | tf_op jit(solution)/shard_map/share_coefficients/ppermute | solution.py:312
  47.4 0.0 collective-permute-done.1.piece2
  47.4 4.8 %collective-permute-start.2 = (f32[8,2,32,128]{3,2,1,0:T(8,128)S(1)}, f32[8,2,32,128]{3,2,1,0:T(8,128)S(1)}, u32[]{:S(2)}, u32[]{:S(2)}) collective-permute-start(f32[8,2,32,128]{3,2,1,0:T(8,128)S(1)} %collective-permute-done.1.piece2), channel_id=1, source_target_pairs={{0,8},{8,0},{16,24},{24,16},{32,40},{40,32},{48,56},{56,48},{64,72... | collective-permute-start | bytes 786440 | tf_op jit(solution)/shard_map/share_coefficients/ppermute | solution.py:313
  52.3 0.1 pad_add_fusion.where
  52.4 0.0 collective-permute-done.piece1
  52.4 1.0 collective-permute-done.2.piece3
  53.4 7.5 %fine_spans.1 = (f32[32,32,128]{2,1,0:T(8,128)}, f32[4,32,128]{2,1,0:T(8,128)S(1)}, f32[4,32,128]{2,1,0:T(8,128)S(1)}, f32[8,8,32,128]{3,2,1,0:T(8,128)S(1)}) custom-call(s32[3]{0:T(128)S(1)} %pad_add_fusion.where, f32[8,6,32,128]{3,2,1,0:T(8,128)S(1)} %bitcast.30, f32[8,2,32,128]{3,2,1,0:T(8,128)S(1)} %collective-permute-done.piece1, ...), custom_call_target="tpu_custom_call" | custom-call | flops 42467328 | bytes 94371840 | tf_op jit(solution)/shard_map/fine_spans/pallas_call | solution.py:246
  61.0 0.0 all-gather.5.cloned.1.call-update
  61.0 3.4 %collective-permute-start.4 = (f32[4,32,128]{2,1,0:T(8,128)S(1)}, f32[4,32,128]{2,1,0:T(8,128)S(1)}, u32[]{:S(2)}, u32[]{:S(2)}) collective-permute-start(f32[4,32,128]{2,1,0:T(8,128)S(1)} %get-tuple-element.24), channel_id=1, source_target_pairs={{0,8},{8,16},{16,24},{24,32},{32,40},{40,48},{48,56},{56,64},{64,7... | collective-permute-start | bytes 196616 | tf_op jit(solution)/shard_map/residual/ppermute | solution.py:324
  64.4 3.1 %collective-permute-start.3 = (f32[4,32,128]{2,1,0:T(8,128)S(1)}, f32[4,32,128]{2,1,0:T(8,128)S(1)}, u32[]{:S(2)}, u32[]{:S(2)}) collective-permute-start(f32[4,32,128]{2,1,0:T(8,128)S(1)} %get-tuple-element.23), channel_id=1, source_target_pairs={{0,16},{8,24},{16,32},{24,40},{32,48},{40,56},{48,64},{56,72},{64,... | collective-permute-start | bytes 196616 | tf_op jit(solution)/shard_map/residual/ppermute | solution.py:325
  67.5 20.4 %all-gather.1 = f32[32,32,128]{2,1,0:T(8,128)S(1)} all-gather(f32[4,32,128]{2,1,0:T(8,128)} %param.5), channel_id=3, replica_groups=mesh['tm'=64,'gz'=8] {'gz'}, dimensions={0}, use_global_device_ids=true | all-gather | bytes 589824 | tf_op jit(solution)/shard_map/first_intervals/all_gather | solution.py:321
  87.9 7.5 %first_intervals.1 = (f32[36,32,128]{2,1,0:T(8,128)S(1)}, f32[2,4,32,128]{3,2,1,0:T(8,128)S(1)}) custom-call(s32[3]{0:T(128)S(1)} %pad_add_fusion.where, f32[8,8,32,128]{3,2,1,0:T(8,128)S(1)} %get-tuple-element.18.fields, f32[8,4,32,128]{3,2,1,0:T(8,128)S(1)} %bitcast.31), custom_call_target="tpu_custom_call" | custom-call | flops 47185920 | bytes 104857600 | tf_op jit(solution)/shard_map/first_intervals/pallas_call | solution.py:263
  95.4 0.7 fusion.3
  96.1 20.3 %all-gather.5.cloned.1.call-done = f32[512,32,128]{2,1,0:T(8,128)} async-done(((f32[32,32,128]{2,1,0:T(8,128)}), f32[512,32,128]{2,1,0:T(8,128)}) %all-gather.5.cloned.1.call-update) | async-done | bytes 8388624 | tf_op jit(solution)/shard_map/gather_forcing/all_gather | solution.py:318
  116.4 7.5 %chain.4 = (f32[36,32,128]{2,1,0:T(8,128)S(1)}, f32[4,4,32,128]{3,2,1,0:T(8,128)S(1)}) custom-call(s32[3]{0:T(128)S(1)} %pad_add_fusion.where, f32[8,8,32,128]{3,2,1,0:T(8,128)S(1)} %get-tuple-element.18.fields, f32[36,32,128]{2,1,0:T(8,128)S(1)} %get-tuple-element.25.message, f32[16,32,32,128]{3,2,1,0:T(8,128)} %bitcast.32), custom_call_target="tpu_custom_call" | custom-call | flops 37748736 | bytes 83886080 | tf_op jit(solution)/shard_map/chain/pallas_call | solution.py:276
  123.9 0.7 collective-permute-start.5
  124.6 0.0 collective-permute-done.5.message
  124.6 7.5 %chain.5 = (f32[36,32,128]{2,1,0:T(8,128)S(1)}, f32[4,4,32,128]{3,2,1,0:T(8,128)S(1)}) custom-call(s32[3]{0:T(128)S(1)} %pad_add_fusion.where, f32[8,8,32,128]{3,2,1,0:T(8,128)S(1)} %get-tuple-element.18.fields, f32[36,32,128]{2,1,0:T(8,128)S(1)} %collective-permute-done.5.message, f32[16,32,32,128]{3,2,1,0:T(8,128)} %bitcast.33), custom_call_target="tpu_custom_call" | custom-call | flops 37748736 | bytes 83886080 | tf_op jit(solution)/shard_map/chain/pallas_call | solution.py:276
  132.1 0.7 collective-permute-start.6
  132.9 7.5 %chain.6 = (f32[36,32,128]{2,1,0:T(8,128)S(1)}, f32[4,4,32,128]{3,2,1,0:T(8,128)S(1)}) custom-call(s32[3]{0:T(128)S(1)} %pad_add_fusion.where, f32[8,8,32,128]{3,2,1,0:T(8,128)S(1)} %get-tuple-element.18.fields, f32[36,32,128]{2,1,0:T(8,128)S(1)} %collective-permute-done.6.message, f32[16,32,32,128]{3,2,1,0:T(8,128)} %bitcast.34), custom_call_target="tpu_custom_call" | custom-call | flops 37748736 | bytes 83886080 | tf_op jit(solution)/shard_map/chain/pallas_call | solution.py:276
  140.4 0.7 collective-permute-start.7
  141.1 7.5 %chain.7 = f32[4,4,32,128]{3,2,1,0:T(8,128)S(1)} custom-call(s32[3]{0:T(128)S(1)} %pad_add_fusion.where, f32[8,8,32,128]{3,2,1,0:T(8,128)S(1)} %get-tuple-element.18.fields, f32[36,32,128]{2,1,0:T(8,128)S(1)} %collective-permute-done.7.message, f32[16,32,32,128]{3,2,1,0:T(8,128)} %bitcast.35), custom_call_target="tpu_custom_call" | custom-call | flops 37748736 | bytes 83886080 | tf_op jit(solution)/shard_map/chain/pallas_call | solution.py:276
  148.6 0.1 select_select_fusion
  148.7 0.7 collective-permute-start.8
  149.5 1.3 collective-permute-start.9
  150.8 37.6 %collective-permute-done.9 = f32[4,32,128]{2,1,0:T(8,128)S(1)} collective-permute-done((f32[4,32,128]{2,1,0:T(8,128)S(1)}, f32[4,32,128]{2,1,0:T(8,128)S(1)}, u32[]{:S(2)}, u32[]{:S(2)}) %collective-permute-start.9) | collective-permute-done | bytes 65568 | tf_op jit(solution)/shard_map/spread_results/ppermute | solution.py:347
  188.4 0.6 fusion.1
  (9 shorter events, 0.1 us)
Async XLA Ops:
  7.2 109.2 %all-gather.5.cloned.1.call-start = ((), (), s32[]{:S(2)}) async-start(), calls=%async_computation | async-start | bytes 8912896 | tf_op jit(solution)/shard_map/gather_forcing/all_gather | solution.py:318
  36.2 11.2 %collective-permute-start.1 = (f32[8,2,32,128]{3,2,1,0:T(8,128)S(1)}, f32[8,2,32,128]{3,2,1,0:T(8,128)S(1)}, u32[]{:S(2)}, u32[]{:S(2)}) collective-permute-start(f32[8,2,32,128]{3,2,1,0:T(8,128)S(1)} %slice.45), channel_id=1, source_target_pairs={{0,16},{8,24},{16,0},{24,8},{32,48},{40,56},{48,32},{56,40},{64,80... | collective-permute-start | bytes 786440 | tf_op jit(solution)/shard_map/share_coefficients/ppermute | solution.py:311
  39.3 13.0 %collective-permute-start = (f32[8,2,32,128]{3,2,1,0:T(8,128)S(1)}, f32[8,2,32,128]{3,2,1,0:T(8,128)S(1)}, u32[]{:S(2)}, u32[]{:S(2)}) collective-permute-start(f32[8,2,32,128]{3,2,1,0:T(8,128)S(1)} %slice.45), channel_id=1, source_target_pairs={{0,8},{8,0},{16,24},{24,16},{32,40},{40,32},{48,56},{56,48},{64,72... | collective-permute-start | bytes 786440 | tf_op jit(solution)/shard_map/share_coefficients/ppermute | solution.py:312
  47.4 6.0 %collective-permute-start.2 = (f32[8,2,32,128]{3,2,1,0:T(8,128)S(1)}, f32[8,2,32,128]{3,2,1,0:T(8,128)S(1)}, u32[]{:S(2)}, u32[]{:S(2)}) collective-permute-start(f32[8,2,32,128]{3,2,1,0:T(8,128)S(1)} %collective-permute-done.1.piece2), channel_id=1, source_target_pairs={{0,8},{8,0},{16,24},{24,16},{32,40},{40,32},{48,56},{56,48},{64,72... | collective-permute-start | bytes 786440 | tf_op jit(solution)/shard_map/share_coefficients/ppermute | solution.py:313
  61.0 34.4 %collective-permute-start.4 = (f32[4,32,128]{2,1,0:T(8,128)S(1)}, f32[4,32,128]{2,1,0:T(8,128)S(1)}, u32[]{:S(2)}, u32[]{:S(2)}) collective-permute-start(f32[4,32,128]{2,1,0:T(8,128)S(1)} %get-tuple-element.24), channel_id=1, source_target_pairs={{0,8},{8,16},{16,24},{24,32},{32,40},{40,48},{48,56},{56,64},{64,7... | collective-permute-start | bytes 196616 | tf_op jit(solution)/shard_map/residual/ppermute | solution.py:324
  64.4 31.0 %collective-permute-start.3 = (f32[4,32,128]{2,1,0:T(8,128)S(1)}, f32[4,32,128]{2,1,0:T(8,128)S(1)}, u32[]{:S(2)}, u32[]{:S(2)}) collective-permute-start(f32[4,32,128]{2,1,0:T(8,128)S(1)} %get-tuple-element.23), channel_id=1, source_target_pairs={{0,16},{8,24},{16,32},{24,40},{32,48},{40,56},{48,64},{56,72},{64,... | collective-permute-start | bytes 196616 | tf_op jit(solution)/shard_map/residual/ppermute | solution.py:325
  123.9 0.7 collective-permute-start.5
  132.1 0.7 collective-permute-start.6
  140.4 0.7 collective-permute-start.7
  148.7 0.7 collective-permute-start.8
  149.5 38.9 %collective-permute-start.9 = (f32[4,32,128]{2,1,0:T(8,128)S(1)}, f32[4,32,128]{2,1,0:T(8,128)S(1)}, u32[]{:S(2)}, u32[]{:S(2)}) collective-permute-start(f32[4,32,128]{2,1,0:T(8,128)S(1)} %slice_bitcast_fusion), channel_id=1, source_target_pairs={{0,8},{16,24},{32,40},{48,56},{64,72},{80,88},{96,104},{112,120},{... | collective-permute-start | bytes 196616 | tf_op jit(solution)/shard_map/spread_results/ppermute | solution.py:347
Sparse Core Ops, SparseCore 0:
  61.1 55.2 all-gather.4

commit v4 on v3

--- a/solution.py
+++ b/solution.py
@@ -12,7 +12,7 @@
 COARSE_STEP = FINE_STEP * STEPS
 NZ, NX, NY = 32, 32, 128
 SLAB = 4
-SHARE = 2
+SHARE = 3
 GROUP = 16
 ROW = 8
 VMEM_BYTES = 48 * 1024 * 1024
@@ -117,14 +117,17 @@
     return lambda z: fields[SLAB + z % SLAB, z // SLAB]
 
 
-def fine_kernel(where, gathered, piece1, piece2, piece3, forcing, u_out, w_out, fields, a, b, *coefs):
+def fine_kernel(where, gathered, crossed, twin, twin_crossed, forcing, u_out, w_out, fields, a, b, *coefs):
     first = where[0] * SLAB
-    quarter = where[2]
+    core = where[2]
+    chip = where[3]
     for slab in range(NZ // SLAB):
-        for i in range(SHARE):
-            fields[SHARE * quarter + i, slab] = gathered[slab, SLAB + i]
-            for j, piece in enumerate((piece1, piece2, piece3)):
-                fields[SHARE * (quarter ^ (j + 1)) + i, slab] = piece[slab, i]
+        for owner, own, other in ((core, gathered.at[slab, SLAB:], crossed), (1 - core, twin.at[slab], twin_crossed)):
+            low, high = 3 * owner + 2, 6 + owner
+            fields[3 * owner, slab] = own[0]
+            fields[3 * owner + 1, slab] = own[1]
+            fields[jnp.where(chip == 0, low, high), slab] = own[2]
+            fields[jnp.where(chip == 0, high, low), slab] = other[slab, 0]
     clear_edges(a)
     clear_edges(b)
     build(a, coefs, kappa_of(fields), growth_of(fields), FINE_STEP)
@@ -296,23 +299,23 @@
     core = rank % 2
     place = rank % GROUP
     half = GROUP // 2
-    quarter = rank % 4
-    where = jnp.stack([z_rank, place, quarter]).astype(jnp.int32)
+    chip = rank // 2 % 2
+    where = jnp.stack([z_rank, place, core, chip]).astype(jnp.int32)
     across = [(i, i ^ 2) for i in range(count)]
     swap = [(i, i ^ 1) for i in range(count)]
 
     with jax.named_scope("gather_fields"):
-        low = jnp.where(quarter % 2 == 0, diffusivity[:SHARE], diffusivity[SHARE:])
-        high = jnp.where(quarter % 2 == 0, growth_rate[:SHARE], growth_rate[SHARE:])
-        share = jnp.where(quarter < 2, low, high)
-        gathered = lax.all_gather(jnp.concatenate([cpoint_guess[0], share]), "gz")
+        pair = jnp.where(core == 0, diffusivity[:2], jnp.concatenate([diffusivity[3:], growth_rate[:1]]))
+        low = jnp.where(core == 0, diffusivity[2:3], growth_rate[1:2])
+        high = jnp.where(core == 0, growth_rate[2:3], growth_rate[3:])
+        third = jnp.where(chip == 0, low, high)
+        gathered = lax.all_gather(jnp.concatenate([cpoint_guess[0], pair, third]), "gz")
     with jax.named_scope("share_coefficients"):
-        share = gathered[:, SLAB:]
-        piece2 = lax.ppermute(share, "tm", across)
-        piece1 = lax.ppermute(share, "tm", swap)
-        piece3 = lax.ppermute(piece2, "tm", swap)
+        crossed = lax.ppermute(gathered[:, SLAB + 2 :], "tm", across)
+        twin = lax.ppermute(gathered[:, SLAB:], "tm", swap)
+        twin_crossed = lax.ppermute(crossed, "tm", swap)
     with jax.named_scope("fine_spans"):
-        forcing, u_slab, w_slab, fields = run_fine(where, gathered, (piece1, piece2, piece3))
+        forcing, u_slab, w_slab, fields = run_fine(where, gathered, (crossed, twin, twin_crossed))
     with jax.named_scope("gather_forcing"):
         members = [[GROUP * g + i for i in range(GROUP)] for g in range(groups)]
         forcing = lax.all_gather(forcing, "tm", axis_index_groups=members)

time: 196 us -> 199 us (1.015)
  waiting for transfers between devices: 59 us -> 63.1 us
  starting transfers between devices: 26.6 us -> 24.1 us
    ppermute x3, waiting for transfers between devices: 1.05 us -> 4.75 us  [the longest x1 3.88 us: shards(): crossed = lax.ppermute(gathered[:, SLAB + 2:], 'tm', across)]
    ppermute x3, starting transfers between devices: 16 us -> 13.6 us  [the longest x1 7.76 us: shards(): twin = lax.ppermute(gathered[:, SLAB:], 'tm', swap)]
  transfers between devices with their start and end apart: 11 -> 11, of which waited for: 3 -> 4; matrix products, arithmetic and copies ran while one was open for 0% -> 0% of each run, Pallas kernels for 4% -> 4%
where the time goes in v4:
time: 199 us; the launch traced here: 198 us
  waiting for transfers between devices  63.1 us (32%)
  blocking collectives  47.7 us (24%)
  Pallas kernels  45.1 us (23%)
  starting transfers between devices  24.1 us (12%)
  between operations  14.3 us (7%)
  other arithmetic  3.92 us (2%)
    ppermute x1, waiting for transfers between devices, shards(): odd = lax.ppermute(pair[1], 'tm', [(i, i + 1) for i in range(0, count, 2)])  37.6 us
    pallas_call x4, Pallas kernels, run_chain(): pl.pallas_call(functools.partial(chain_kernel, last), out_shape=outs, in_...  30 us
    all_gather x1, blocking collectives, shards(): lax.all_gather(jnp.concatenate([cpoint_guess[0], pair, third]), 'gz')  27.6 us
    all_gather x1, waiting for transfers between devices, shards(): forcing = lax.all_gather(forcing, 'tm', axis_index_groups=members)  20.7 us
    all_gather x1, blocking collectives, shards(): initial = lax.all_gather(initial, 'gz')  20 us
    ppermute x1, starting transfers between devices, shards(): twin = lax.ppermute(gathered[:, SLAB:], 'tm', swap)  7.76 us
    pallas_call x1, Pallas kernels, run_fine(): pl.pallas_call(fine_kernel, out_shape=[f32(NZ, *PLANE), f32(SLAB, *PLANE)...  7.54 us
    pallas_call x1, Pallas kernels, run_start(): pl.pallas_call(start_kernel, out_shape=[f32(MESSAGE, *PLANE), f32(2, SLAB...  7.5 us
  transfers between devices with their start and end apart: 11, of which 4 were waited for; matrix products, arithmetic and copies ran while one was open for 0% of the time, Pallas kernels for 4%

profile of v4, /device:TPU:57, one launch (start us, length us, event | category | flops | bytes accessed | tf_op | source)
XLA Modules:
  0.0 198.3 jit_solution(12999553211594581979)
XLA Ops:
  7.2 0.0 all-gather.5.cloned.1.call-start
  7.3 0.8 fusion.4
  8.1 0.8 maximum_select_fusion
  8.8 0.8 pad_maximum_fusion
  9.7 27.6 %all-gather = f32[56,32,128]{2,1,0:T(8,128)S(1)} all-gather(f32[7,32,128]{2,1,0:T(8,128)S(1)} %pad_maximum_fusion), channel_id=2, replica_groups=mesh['tm'=64,'gz'=8] {'gz'}, dimensions={0}, use_global_device_ids=true | all-gather | bytes 1032192 | tf_op jit(solution)/shard_map/gather_fields/all_gather | solution.py:312
  37.3 7.8 %collective-permute-start.1 = (f32[8,3,32,128]{3,2,1,0:T(8,128)S(1)}, f32[8,3,32,128]{3,2,1,0:T(8,128)S(1)}, u32[]{:S(2)}, u32[]{:S(2)}) collective-permute-start(f32[8,3,32,128]{3,2,1,0:T(8,128)S(1)} %slice.62), channel_id=1, source_target_pairs={{0,8},{8,0},{16,24},{24,16},{32,40},{40,32},{48,56},{56,48},{64,72... | collective-permute-start | bytes 1179656 | tf_op jit(solution)/shard_map/share_coefficients/ppermute | solution.py:315
  45.1 3.1 %collective-permute-start = (f32[8,1,32,128]{3,2,1,0:T(8,128)S(1)}, f32[8,1,32,128]{3,2,1,0:T(8,128)S(1)}, u32[]{:S(2)}, u32[]{:S(2)}) collective-permute-start(f32[8,1,32,128]{3,2,1,0:T(8,128)S(1)} %slice.61), channel_id=1, source_target_pairs={{0,16},{8,24},{16,0},{24,8},{32,48},{40,56},{48,32},{56,40},{64,80... | collective-permute-start | bytes 393224 | tf_op jit(solution)/shard_map/share_coefficients/ppermute | solution.py:314
  48.3 3.9 %collective-permute-done.crossed = f32[8,1,32,128]{3,2,1,0:T(8,128)S(1)} collective-permute-done((f32[8,1,32,128]{3,2,1,0:T(8,128)S(1)}, f32[8,1,32,128]{3,2,1,0:T(8,128)S(1)}, u32[]{:S(2)}, u32[]{:S(2)}) %collective-permute-start) | collective-permute-done | bytes 131104 | tf_op jit(solution)/shard_map/share_coefficients/ppermute | solution.py:314
  52.1 2.7 %collective-permute-start.2 = (f32[8,1,32,128]{3,2,1,0:T(8,128)S(1)}, f32[8,1,32,128]{3,2,1,0:T(8,128)S(1)}, u32[]{:S(2)}, u32[]{:S(2)}) collective-permute-start(f32[8,1,32,128]{3,2,1,0:T(8,128)S(1)} %collective-permute-done.crossed), channel_id=1, source_target_pairs={{0,8},{8,0},{16,24},{24,16},{32,40},{40,32},{48,56},{56,48},{64,72... | collective-permute-start | bytes 393224 | tf_op jit(solution)/shard_map/share_coefficients/ppermute | solution.py:316
  54.9 0.1 pad_add_fusion.where
  54.9 0.9 collective-permute-done.2.twin_crossed
  55.8 0.0 collective-permute-done.1.twin
  55.8 7.5 %fine_spans.1 = (f32[32,32,128]{2,1,0:T(8,128)}, f32[4,32,128]{2,1,0:T(8,128)S(1)}, f32[4,32,128]{2,1,0:T(8,128)S(1)}, f32[8,8,32,128]{3,2,1,0:T(8,128)S(1)}) custom-call(s32[4]{0:T(128)S(1)} %pad_add_fusion.where, f32[8,7,32,128]{3,2,1,0:T(8,128)S(1)} %bitcast.32, f32[8,1,32,128]{3,2,1,0:T(8,128)S(1)} %collective-permute-done.crossed, ...), custom_call_target="tpu_custom_call" | custom-call | flops 42467328 | bytes 94371840 | tf_op jit(solution)/shard_map/fine_spans/pallas_call | solution.py:249
  63.3 0.0 all-gather.5.cloned.1.call-update
  63.4 3.4 %collective-permute-start.4 = (f32[4,32,128]{2,1,0:T(8,128)S(1)}, f32[4,32,128]{2,1,0:T(8,128)S(1)}, u32[]{:S(2)}, u32[]{:S(2)}) collective-permute-start(f32[4,32,128]{2,1,0:T(8,128)S(1)} %get-tuple-element.24), channel_id=1, source_target_pairs={{0,8},{8,16},{16,24},{24,32},{32,40},{40,48},{48,56},{56,64},{64,7... | collective-permute-start | bytes 196616 | tf_op jit(solution)/shard_map/residual/ppermute | solution.py:327
  66.8 3.1 %collective-permute-start.3 = (f32[4,32,128]{2,1,0:T(8,128)S(1)}, f32[4,32,128]{2,1,0:T(8,128)S(1)}, u32[]{:S(2)}, u32[]{:S(2)}) collective-permute-start(f32[4,32,128]{2,1,0:T(8,128)S(1)} %get-tuple-element.23), channel_id=1, source_target_pairs={{0,16},{8,24},{16,32},{24,40},{32,48},{40,56},{48,64},{56,72},{64,... | collective-permute-start | bytes 196616 | tf_op jit(solution)/shard_map/residual/ppermute | solution.py:328
  69.9 20.0 %all-gather.1 = f32[32,32,128]{2,1,0:T(8,128)S(1)} all-gather(f32[4,32,128]{2,1,0:T(8,128)} %param.5), channel_id=3, replica_groups=mesh['tm'=64,'gz'=8] {'gz'}, dimensions={0}, use_global_device_ids=true | all-gather | bytes 589824 | tf_op jit(solution)/shard_map/first_intervals/all_gather | solution.py:324
  89.9 7.5 %first_intervals.1 = (f32[36,32,128]{2,1,0:T(8,128)S(1)}, f32[2,4,32,128]{3,2,1,0:T(8,128)S(1)}) custom-call(s32[4]{0:T(128)S(1)} %pad_add_fusion.where, f32[8,8,32,128]{3,2,1,0:T(8,128)S(1)} %get-tuple-element.18.fields, f32[8,4,32,128]{3,2,1,0:T(8,128)S(1)} %bitcast.33), custom_call_target="tpu_custom_call" | custom-call | flops 47185920 | bytes 104857600 | tf_op jit(solution)/shard_map/first_intervals/pallas_call | solution.py:266
  97.4 0.7 fusion.3
  98.1 20.7 %all-gather.5.cloned.1.call-done = f32[512,32,128]{2,1,0:T(8,128)} async-done(((f32[32,32,128]{2,1,0:T(8,128)}), f32[512,32,128]{2,1,0:T(8,128)}) %all-gather.5.cloned.1.call-update) | async-done | bytes 8388624 | tf_op jit(solution)/shard_map/gather_forcing/all_gather | solution.py:321
  118.8 7.5 %chain.4 = (f32[36,32,128]{2,1,0:T(8,128)S(1)}, f32[4,4,32,128]{3,2,1,0:T(8,128)S(1)}) custom-call(s32[4]{0:T(128)S(1)} %pad_add_fusion.where, f32[8,8,32,128]{3,2,1,0:T(8,128)S(1)} %get-tuple-element.18.fields, f32[36,32,128]{2,1,0:T(8,128)S(1)} %get-tuple-element.25.message, f32[16,32,32,128]{3,2,1,0:T(8,128)} %bitcast.34), custom_call_target="tpu_custom_call" | custom-call | flops 37748736 | bytes 83886080 | tf_op jit(solution)/shard_map/chain/pallas_call | solution.py:279
  126.3 0.7 collective-permute-start.5
  127.0 7.5 %chain.5 = (f32[36,32,128]{2,1,0:T(8,128)S(1)}, f32[4,4,32,128]{3,2,1,0:T(8,128)S(1)}) custom-call(s32[4]{0:T(128)S(1)} %pad_add_fusion.where, f32[8,8,32,128]{3,2,1,0:T(8,128)S(1)} %get-tuple-element.18.fields, f32[36,32,128]{2,1,0:T(8,128)S(1)} %collective-permute-done.5.message, f32[16,32,32,128]{3,2,1,0:T(8,128)} %bitcast.35), custom_call_target="tpu_custom_call" | custom-call | flops 37748736 | bytes 83886080 | tf_op jit(solution)/shard_map/chain/pallas_call | solution.py:279
  134.6 0.7 collective-permute-start.6
  135.3 7.5 %chain.6 = (f32[36,32,128]{2,1,0:T(8,128)S(1)}, f32[4,4,32,128]{3,2,1,0:T(8,128)S(1)}) custom-call(s32[4]{0:T(128)S(1)} %pad_add_fusion.where, f32[8,8,32,128]{3,2,1,0:T(8,128)S(1)} %get-tuple-element.18.fields, f32[36,32,128]{2,1,0:T(8,128)S(1)} %collective-permute-done.6.message, f32[16,32,32,128]{3,2,1,0:T(8,128)} %bitcast.36), custom_call_target="tpu_custom_call" | custom-call | flops 37748736 | bytes 83886080 | tf_op jit(solution)/shard_map/chain/pallas_call | solution.py:279
  142.8 0.7 collective-permute-start.7
  143.5 7.5 %chain.7 = f32[4,4,32,128]{3,2,1,0:T(8,128)S(1)} custom-call(s32[4]{0:T(128)S(1)} %pad_add_fusion.where, f32[8,8,32,128]{3,2,1,0:T(8,128)S(1)} %get-tuple-element.18.fields, f32[36,32,128]{2,1,0:T(8,128)S(1)} %collective-permute-done.7.message, f32[16,32,32,128]{3,2,1,0:T(8,128)} %bitcast.37), custom_call_target="tpu_custom_call" | custom-call | flops 37748736 | bytes 83886080 | tf_op jit(solution)/shard_map/chain/pallas_call | solution.py:279
  151.0 0.1 select_select_fusion
  151.1 0.7 collective-permute-start.8
  151.9 1.3 collective-permute-start.9
  153.2 37.6 %collective-permute-done.9 = f32[4,32,128]{2,1,0:T(8,128)S(1)} collective-permute-done((f32[4,32,128]{2,1,0:T(8,128)S(1)}, f32[4,32,128]{2,1,0:T(8,128)S(1)}, u32[]{:S(2)}, u32[]{:S(2)}) %collective-permute-start.9) | collective-permute-done | bytes 65568 | tf_op jit(solution)/shard_map/spread_results/ppermute | solution.py:350
  190.8 0.6 fusion.1
  (11 shorter events, 0.1 us)
Async XLA Ops:
  7.2 111.6 %all-gather.5.cloned.1.call-start = ((), (), s32[]{:S(2)}) async-start(), calls=%async_computation | async-start | bytes 8912896 | tf_op jit(solution)/shard_map/gather_forcing/all_gather | solution.py:321
  37.3 18.5 %collective-permute-start.1 = (f32[8,3,32,128]{3,2,1,0:T(8,128)S(1)}, f32[8,3,32,128]{3,2,1,0:T(8,128)S(1)}, u32[]{:S(2)}, u32[]{:S(2)}) collective-permute-start(f32[8,3,32,128]{3,2,1,0:T(8,128)S(1)} %slice.62), channel_id=1, source_target_pairs={{0,8},{8,0},{16,24},{24,16},{32,40},{40,32},{48,56},{56,48},{64,72... | collective-permute-start | bytes 1179656 | tf_op jit(solution)/shard_map/share_coefficients/ppermute | solution.py:315
  45.1 7.0 %collective-permute-start = (f32[8,1,32,128]{3,2,1,0:T(8,128)S(1)}, f32[8,1,32,128]{3,2,1,0:T(8,128)S(1)}, u32[]{:S(2)}, u32[]{:S(2)}) collective-permute-start(f32[8,1,32,128]{3,2,1,0:T(8,128)S(1)} %slice.61), channel_id=1, source_target_pairs={{0,16},{8,24},{16,0},{24,8},{32,48},{40,56},{48,32},{56,40},{64,80... | collective-permute-start | bytes 393224 | tf_op jit(solution)/shard_map/share_coefficients/ppermute | solution.py:314
  52.1 3.7 %collective-permute-start.2 = (f32[8,1,32,128]{3,2,1,0:T(8,128)S(1)}, f32[8,1,32,128]{3,2,1,0:T(8,128)S(1)}, u32[]{:S(2)}, u32[]{:S(2)}) collective-permute-start(f32[8,1,32,128]{3,2,1,0:T(8,128)S(1)} %collective-permute-done.crossed), channel_id=1, source_target_pairs={{0,8},{8,0},{16,24},{24,16},{32,40},{40,32},{48,56},{56,48},{64,72... | collective-permute-start | bytes 393224 | tf_op jit(solution)/shard_map/share_coefficients/ppermute | solution.py:316
  63.4 34.0 %collective-permute-start.4 = (f32[4,32,128]{2,1,0:T(8,128)S(1)}, f32[4,32,128]{2,1,0:T(8,128)S(1)}, u32[]{:S(2)}, u32[]{:S(2)}) collective-permute-start(f32[4,32,128]{2,1,0:T(8,128)S(1)} %get-tuple-element.24), channel_id=1, source_target_pairs={{0,8},{8,16},{16,24},{24,32},{32,40},{40,48},{48,56},{56,64},{64,7... | collective-permute-start | bytes 196616 | tf_op jit(solution)/shard_map/residual/ppermute | solution.py:327
  66.8 30.7 %collective-permute-start.3 = (f32[4,32,128]{2,1,0:T(8,128)S(1)}, f32[4,32,128]{2,1,0:T(8,128)S(1)}, u32[]{:S(2)}, u32[]{:S(2)}) collective-permute-start(f32[4,32,128]{2,1,0:T(8,128)S(1)} %get-tuple-element.23), channel_id=1, source_target_pairs={{0,16},{8,24},{16,32},{24,40},{32,48},{40,56},{48,64},{56,72},{64,... | collective-permute-start | bytes 196616 | tf_op jit(solution)/shard_map/residual/ppermute | solution.py:328
  126.3 0.7 collective-permute-start.5
  134.6 0.7 collective-permute-start.6
  142.8 0.7 collective-permute-start.7
  151.1 0.7 collective-permute-start.8
  151.9 38.9 %collective-permute-start.9 = (f32[4,32,128]{2,1,0:T(8,128)S(1)}, f32[4,32,128]{2,1,0:T(8,128)S(1)}, u32[]{:S(2)}, u32[]{:S(2)}) collective-permute-start(f32[4,32,128]{2,1,0:T(8,128)S(1)} %slice_bitcast_fusion), channel_id=1, source_target_pairs={{0,8},{16,24},{32,40},{48,56},{64,72},{80,88},{96,104},{112,120},{... | collective-permute-start | bytes 196616 | tf_op jit(solution)/shard_map/spread_results/ppermute | solution.py:350
Sparse Core Ops, SparseCore 0:
  63.5 55.2 all-gather.4

commit v5 on v3

--- a/solution.py
+++ b/solution.py
@@ -15,6 +15,7 @@
 SHARE = 2
 GROUP = 16
 ROW = 8
+AHEAD = 3
 VMEM_BYTES = 48 * 1024 * 1024
 
 PLANE = (NX, NY)
@@ -177,7 +178,7 @@
     def copy_of(index):
         return pltpu.make_async_copy(gathered_forcing.at[index], forcing.at[index], sems.at[index])
 
-    for index in range(GROUP):
+    for index in range(AHEAD):
         copy_of(index).start()
 
     clear_edges(a)
@@ -193,6 +194,10 @@
             picked[1, i] = get(a, first + i)
 
     def advance(src, dst, index):
+        @pl.when(index + AHEAD < GROUP)
+        def _():
+            copy_of(index + AHEAD).start()
+
         copy_of(index).wait()
         step(src, dst, coefs, finish=lambda z, value: value + forcing[index, z])
 

time: 196 us -> 197 us (level)
  no operation moved by 1% of the time
where the time goes in v5:
time: 197 us; the launch traced here: 196 us
  waiting for transfers between devices  59 us (30%)
  blocking collectives  47.7 us (24%)
  Pallas kernels  45.7 us (23%)
  starting transfers between devices  26.6 us (14%)
  between operations  14.3 us (7%)
  other arithmetic  3.16 us (2%)
    ppermute x1, waiting for transfers between devices, shards(): odd = lax.ppermute(pair[1], 'tm', [(i, i + 1) for i in range(0, count, 2)])  37.6 us
    pallas_call x4, Pallas kernels, run_chain(): pl.pallas_call(functools.partial(chain_kernel, last), out_shape=outs, in_...  30.6 us
    all_gather x1, blocking collectives, shards(): gathered = lax.all_gather(jnp.concatenate([cpoint_guess[0], share]), 'gz')  27.3 us
    all_gather x1, blocking collectives, shards(): initial = lax.all_gather(initial, 'gz')  20.4 us
    all_gather x1, waiting for transfers between devices, shards(): forcing = lax.all_gather(forcing, 'tm', axis_index_groups=members)  20.3 us
    ppermute x1, starting transfers between devices, shards(): piece1 = lax.ppermute(share, 'tm', swap)  8.09 us
    pallas_call x1, Pallas kernels, run_fine(): pl.pallas_call(fine_kernel, out_shape=[f32(NZ, *PLANE), f32(SLAB, *PLANE)...  7.54 us
    pallas_call x1, Pallas kernels, run_start(): pl.pallas_call(start_kernel, out_shape=[f32(MESSAGE, *PLANE), f32(2, SLAB...  7.5 us
  transfers between devices with their start and end apart: 11, of which 3 were waited for; matrix products, arithmetic and copies ran while one was open for 0% of the time, Pallas kernels for 4%

profile of v5, /device:TPU:57, one launch (start us, length us, event | category | flops | bytes accessed | tf_op | source)
XLA Modules:
  0.0 196.4 jit_solution(2913989772277935016)
XLA Ops:
  7.2 0.0 all-gather.5.cloned.1.call-start
  7.2 0.8 select_select_fusion.1
  8.1 0.8 pad_maximum_fusion
  8.9 27.3 %all-gather = f32[48,32,128]{2,1,0:T(8,128)S(1)} all-gather(f32[6,32,128]{2,1,0:T(8,128)S(1)} %pad_maximum_fusion), channel_id=2, replica_groups=mesh['tm'=64,'gz'=8] {'gz'}, dimensions={0}, use_global_device_ids=true | all-gather | bytes 884736 | tf_op jit(solution)/shard_map/gather_fields/all_gather | solution.py:313
  36.2 3.1 %collective-permute-start.1 = (f32[8,2,32,128]{3,2,1,0:T(8,128)S(1)}, f32[8,2,32,128]{3,2,1,0:T(8,128)S(1)}, u32[]{:S(2)}, u32[]{:S(2)}) collective-permute-start(f32[8,2,32,128]{3,2,1,0:T(8,128)S(1)} %slice.45), channel_id=1, source_target_pairs={{0,16},{8,24},{16,0},{24,8},{32,48},{40,56},{48,32},{56,40},{64,80... | collective-permute-start | bytes 786440 | tf_op jit(solution)/shard_map/share_coefficients/ppermute | solution.py:316
  39.3 8.1 %collective-permute-start = (f32[8,2,32,128]{3,2,1,0:T(8,128)S(1)}, f32[8,2,32,128]{3,2,1,0:T(8,128)S(1)}, u32[]{:S(2)}, u32[]{:S(2)}) collective-permute-start(f32[8,2,32,128]{3,2,1,0:T(8,128)S(1)} %slice.45), channel_id=1, source_target_pairs={{0,8},{8,0},{16,24},{24,16},{32,40},{40,32},{48,56},{56,48},{64,72... | collective-permute-start | bytes 786440 | tf_op jit(solution)/shard_map/share_coefficients/ppermute | solution.py:317
  47.4 0.0 collective-permute-done.1.piece2
  47.4 4.8 %collective-permute-start.2 = (f32[8,2,32,128]{3,2,1,0:T(8,128)S(1)}, f32[8,2,32,128]{3,2,1,0:T(8,128)S(1)}, u32[]{:S(2)}, u32[]{:S(2)}) collective-permute-start(f32[8,2,32,128]{3,2,1,0:T(8,128)S(1)} %collective-permute-done.1.piece2), channel_id=1, source_target_pairs={{0,8},{8,0},{16,24},{24,16},{32,40},{40,32},{48,56},{56,48},{64,72... | collective-permute-start | bytes 786440 | tf_op jit(solution)/shard_map/share_coefficients/ppermute | solution.py:318
  52.3 0.1 pad_add_fusion.where
  52.4 0.0 collective-permute-done.piece1
  52.4 1.0 collective-permute-done.2.piece3
  53.4 7.5 %fine_spans.1 = (f32[32,32,128]{2,1,0:T(8,128)}, f32[4,32,128]{2,1,0:T(8,128)S(1)}, f32[4,32,128]{2,1,0:T(8,128)S(1)}, f32[8,8,32,128]{3,2,1,0:T(8,128)S(1)}) custom-call(s32[3]{0:T(128)S(1)} %pad_add_fusion.where, f32[8,6,32,128]{3,2,1,0:T(8,128)S(1)} %bitcast.30, f32[8,2,32,128]{3,2,1,0:T(8,128)S(1)} %collective-permute-done.piece1, ...), custom_call_target="tpu_custom_call" | custom-call | flops 42467328 | bytes 94371840 | tf_op jit(solution)/shard_map/fine_spans/pallas_call | solution.py:251
  61.0 0.0 all-gather.5.cloned.1.call-update
  61.0 3.4 %collective-permute-start.4 = (f32[4,32,128]{2,1,0:T(8,128)S(1)}, f32[4,32,128]{2,1,0:T(8,128)S(1)}, u32[]{:S(2)}, u32[]{:S(2)}) collective-permute-start(f32[4,32,128]{2,1,0:T(8,128)S(1)} %get-tuple-element.24), channel_id=1, source_target_pairs={{0,8},{8,16},{16,24},{24,32},{32,40},{40,48},{48,56},{56,64},{64,7... | collective-permute-start | bytes 196616 | tf_op jit(solution)/shard_map/residual/ppermute | solution.py:329
  64.4 3.1 %collective-permute-start.3 = (f32[4,32,128]{2,1,0:T(8,128)S(1)}, f32[4,32,128]{2,1,0:T(8,128)S(1)}, u32[]{:S(2)}, u32[]{:S(2)}) collective-permute-start(f32[4,32,128]{2,1,0:T(8,128)S(1)} %get-tuple-element.23), channel_id=1, source_target_pairs={{0,16},{8,24},{16,32},{24,40},{32,48},{40,56},{48,64},{56,72},{64,... | collective-permute-start | bytes 196616 | tf_op jit(solution)/shard_map/residual/ppermute | solution.py:330
  67.5 20.4 %all-gather.1 = f32[32,32,128]{2,1,0:T(8,128)S(1)} all-gather(f32[4,32,128]{2,1,0:T(8,128)} %param.5), channel_id=3, replica_groups=mesh['tm'=64,'gz'=8] {'gz'}, dimensions={0}, use_global_device_ids=true | all-gather | bytes 589824 | tf_op jit(solution)/shard_map/first_intervals/all_gather | solution.py:326
  87.9 7.5 %first_intervals.1 = (f32[36,32,128]{2,1,0:T(8,128)S(1)}, f32[2,4,32,128]{3,2,1,0:T(8,128)S(1)}) custom-call(s32[3]{0:T(128)S(1)} %pad_add_fusion.where, f32[8,8,32,128]{3,2,1,0:T(8,128)S(1)} %get-tuple-element.18.fields, f32[8,4,32,128]{3,2,1,0:T(8,128)S(1)} %bitcast.31), custom_call_target="tpu_custom_call" | custom-call | flops 47185920 | bytes 104857600 | tf_op jit(solution)/shard_map/first_intervals/pallas_call | solution.py:268
  95.4 0.7 fusion.3
  96.1 20.3 %all-gather.5.cloned.1.call-done = f32[512,32,128]{2,1,0:T(8,128)} async-done(((f32[32,32,128]{2,1,0:T(8,128)}), f32[512,32,128]{2,1,0:T(8,128)}) %all-gather.5.cloned.1.call-update) | async-done | bytes 8388624 | tf_op jit(solution)/shard_map/gather_forcing/all_gather | solution.py:323
  116.4 7.7 %chain.4 = (f32[36,32,128]{2,1,0:T(8,128)S(1)}, f32[4,4,32,128]{3,2,1,0:T(8,128)S(1)}) custom-call(s32[3]{0:T(128)S(1)} %pad_add_fusion.where, f32[8,8,32,128]{3,2,1,0:T(8,128)S(1)} %get-tuple-element.18.fields, f32[36,32,128]{2,1,0:T(8,128)S(1)} %get-tuple-element.25.message, f32[16,32,32,128]{3,2,1,0:T(8,128)} %bitcast.32), custom_call_target="tpu_custom_call" | custom-call | flops 37748736 | bytes 83886080 | tf_op jit(solution)/shard_map/chain/pallas_call | solution.py:281
  124.0 0.7 collective-permute-start.5
  124.8 0.0 collective-permute-done.5.message
  124.8 7.7 %chain.5 = (f32[36,32,128]{2,1,0:T(8,128)S(1)}, f32[4,4,32,128]{3,2,1,0:T(8,128)S(1)}) custom-call(s32[3]{0:T(128)S(1)} %pad_add_fusion.where, f32[8,8,32,128]{3,2,1,0:T(8,128)S(1)} %get-tuple-element.18.fields, f32[36,32,128]{2,1,0:T(8,128)S(1)} %collective-permute-done.5.message, f32[16,32,32,128]{3,2,1,0:T(8,128)} %bitcast.33), custom_call_target="tpu_custom_call" | custom-call | flops 37748736 | bytes 83886080 | tf_op jit(solution)/shard_map/chain/pallas_call | solution.py:281
  132.4 0.7 collective-permute-start.6
  133.2 7.7 %chain.6 = (f32[36,32,128]{2,1,0:T(8,128)S(1)}, f32[4,4,32,128]{3,2,1,0:T(8,128)S(1)}) custom-call(s32[3]{0:T(128)S(1)} %pad_add_fusion.where, f32[8,8,32,128]{3,2,1,0:T(8,128)S(1)} %get-tuple-element.18.fields, f32[36,32,128]{2,1,0:T(8,128)S(1)} %collective-permute-done.6.message, f32[16,32,32,128]{3,2,1,0:T(8,128)} %bitcast.34), custom_call_target="tpu_custom_call" | custom-call | flops 37748736 | bytes 83886080 | tf_op jit(solution)/shard_map/chain/pallas_call | solution.py:281
  140.8 0.7 collective-permute-start.7
  141.6 7.6 %chain.7 = f32[4,4,32,128]{3,2,1,0:T(8,128)S(1)} custom-call(s32[3]{0:T(128)S(1)} %pad_add_fusion.where, f32[8,8,32,128]{3,2,1,0:T(8,128)S(1)} %get-tuple-element.18.fields, f32[36,32,128]{2,1,0:T(8,128)S(1)} %collective-permute-done.7.message, f32[16,32,32,128]{3,2,1,0:T(8,128)} %bitcast.35), custom_call_target="tpu_custom_call" | custom-call | flops 37748736 | bytes 83886080 | tf_op jit(solution)/shard_map/chain/pallas_call | solution.py:281
  149.2 0.1 select_select_fusion
  149.3 0.7 collective-permute-start.8
  150.1 1.3 collective-permute-start.9
  151.4 37.6 %collective-permute-done.9 = f32[4,32,128]{2,1,0:T(8,128)S(1)} collective-permute-done((f32[4,32,128]{2,1,0:T(8,128)S(1)}, f32[4,32,128]{2,1,0:T(8,128)S(1)}, u32[]{:S(2)}, u32[]{:S(2)}) %collective-permute-start.9) | collective-permute-done | bytes 65568 | tf_op jit(solution)/shard_map/spread_results/ppermute | solution.py:352
  188.9 0.6 fusion.1
  (9 shorter events, 0.1 us)
Async XLA Ops:
  7.2 109.2 %all-gather.5.cloned.1.call-start = ((), (), s32[]{:S(2)}) async-start(), calls=%async_computation | async-start | bytes 8912896 | tf_op jit(solution)/shard_map/gather_forcing/all_gather | solution.py:323
  36.2 11.2 %collective-permute-start.1 = (f32[8,2,32,128]{3,2,1,0:T(8,128)S(1)}, f32[8,2,32,128]{3,2,1,0:T(8,128)S(1)}, u32[]{:S(2)}, u32[]{:S(2)}) collective-permute-start(f32[8,2,32,128]{3,2,1,0:T(8,128)S(1)} %slice.45), channel_id=1, source_target_pairs={{0,16},{8,24},{16,0},{24,8},{32,48},{40,56},{48,32},{56,40},{64,80... | collective-permute-start | bytes 786440 | tf_op jit(solution)/shard_map/share_coefficients/ppermute | solution.py:316
  39.3 13.0 %collective-permute-start = (f32[8,2,32,128]{3,2,1,0:T(8,128)S(1)}, f32[8,2,32,128]{3,2,1,0:T(8,128)S(1)}, u32[]{:S(2)}, u32[]{:S(2)}) collective-permute-start(f32[8,2,32,128]{3,2,1,0:T(8,128)S(1)} %slice.45), channel_id=1, source_target_pairs={{0,8},{8,0},{16,24},{24,16},{32,40},{40,32},{48,56},{56,48},{64,72... | collective-permute-start | bytes 786440 | tf_op jit(solution)/shard_map/share_coefficients/ppermute | solution.py:317
  47.4 6.0 %collective-permute-start.2 = (f32[8,2,32,128]{3,2,1,0:T(8,128)S(1)}, f32[8,2,32,128]{3,2,1,0:T(8,128)S(1)}, u32[]{:S(2)}, u32[]{:S(2)}) collective-permute-start(f32[8,2,32,128]{3,2,1,0:T(8,128)S(1)} %collective-permute-done.1.piece2), channel_id=1, source_target_pairs={{0,8},{8,0},{16,24},{24,16},{32,40},{40,32},{48,56},{56,48},{64,72... | collective-permute-start | bytes 786440 | tf_op jit(solution)/shard_map/share_coefficients/ppermute | solution.py:318
  61.0 34.4 %collective-permute-start.4 = (f32[4,32,128]{2,1,0:T(8,128)S(1)}, f32[4,32,128]{2,1,0:T(8,128)S(1)}, u32[]{:S(2)}, u32[]{:S(2)}) collective-permute-start(f32[4,32,128]{2,1,0:T(8,128)S(1)} %get-tuple-element.24), channel_id=1, source_target_pairs={{0,8},{8,16},{16,24},{24,32},{32,40},{40,48},{48,56},{56,64},{64,7... | collective-permute-start | bytes 196616 | tf_op jit(solution)/shard_map/residual/ppermute | solution.py:329
  64.4 31.0 %collective-permute-start.3 = (f32[4,32,128]{2,1,0:T(8,128)S(1)}, f32[4,32,128]{2,1,0:T(8,128)S(1)}, u32[]{:S(2)}, u32[]{:S(2)}) collective-permute-start(f32[4,32,128]{2,1,0:T(8,128)S(1)} %get-tuple-element.23), channel_id=1, source_target_pairs={{0,16},{8,24},{16,32},{24,40},{32,48},{40,56},{48,64},{56,72},{64,... | collective-permute-start | bytes 196616 | tf_op jit(solution)/shard_map/residual/ppermute | solution.py:330
  124.0 0.7 collective-permute-start.5
  132.4 0.7 collective-permute-start.6
  140.8 0.7 collective-permute-start.7
  149.3 0.7 collective-permute-start.8
  150.1 38.9 %collective-permute-start.9 = (f32[4,32,128]{2,1,0:T(8,128)S(1)}, f32[4,32,128]{2,1,0:T(8,128)S(1)}, u32[]{:S(2)}, u32[]{:S(2)}) collective-permute-start(f32[4,32,128]{2,1,0:T(8,128)S(1)} %slice_bitcast_fusion), channel_id=1, source_target_pairs={{0,8},{16,24},{32,40},{48,56},{64,72},{80,88},{96,104},{112,120},{... | collective-permute-start | bytes 196616 | tf_op jit(solution)/shard_map/spread_results/ppermute | solution.py:352
Sparse Core Ops, SparseCore 0:
  61.1 55.2 all-gather.4

commit v6 on v3

--- a/solution.py
+++ b/solution.py
@@ -20,7 +20,6 @@
 PLANE = (NX, NY)
 PADDED = (NZ + 2, NX + 16, NY)
 COEFFICIENTS = [(NZ + 1, *PLANE)] + [(NZ, *PLANE)] * 5
-MESSAGE = NZ + SLAB
 
 
 def scratch_set():
@@ -160,8 +159,7 @@
         message[z] = get(a, z) - get(b, z)
         put(a, z, initial[z // SLAB, z % SLAB])
     step(a, b, coefs, scale=scale, finish=lambda z, value: value + (get(c, z) - value))
-    for i in range(SLAB):
-        message[NZ + i] = get(b, first + i)
+    copy_slab(b, first, slabs.at[2])
     step(b, a, coefs, scale=scale, finish=lambda z, value: value + message[z])
     copy_out(a, message)
 
@@ -170,7 +168,7 @@
     if last:
         picked, forcing, sems, a, b, *coefs = refs
     else:
-        message_out, picked, forcing, sems, a, b, *coefs = refs
+        message_out, late, picked, forcing, sems, a, b, *coefs = refs
     first = where[0] * SLAB
     wanted = where[1]
 
@@ -189,7 +187,6 @@
     @pl.when(wanted == 0)
     def _():
         for i in range(SLAB):
-            picked[0, i] = message[NZ + i]
             picked[1, i] = get(a, first + i)
 
     def advance(src, dst, index):
@@ -220,8 +217,7 @@
     lax.fori_loop(0, GROUP // 2, pair, 0)
     if not last:
         copy_out(a, message_out)
-        for i in range(SLAB):
-            message_out[NZ + i] = get(b, first + i)
+        copy_slab(b, first, late)
 
 
 def params():
@@ -262,7 +258,7 @@
 def run_start(where, fields, initial):
     return pl.pallas_call(
         start_kernel,
-        out_shape=[f32(MESSAGE, *PLANE), f32(2, SLAB, *PLANE)],
+        out_shape=[f32(NZ, *PLANE), f32(3, SLAB, *PLANE)],
         in_specs=[SMEM_SPEC, VMEM_SPEC, VMEM_SPEC],
         out_specs=[VMEM_SPEC] * 2,
         scratch_shapes=[pltpu.VMEM(PADDED, jnp.float32)] + scratch_set(),
@@ -272,7 +268,7 @@
 
 
 def run_chain(where, fields, message, forcing, last):
-    outs = ([] if last else [f32(MESSAGE, *PLANE)]) + [f32(4, SLAB, *PLANE)]
+    outs = ([] if last else [f32(NZ, *PLANE), f32(SLAB, *PLANE)]) + [f32(4, SLAB, *PLANE)]
     return pl.pallas_call(
         functools.partial(chain_kernel, last),
         out_shape=outs,
@@ -339,13 +335,18 @@
         if g + 1 < groups:
             with jax.named_scope("hand_over"):
                 hosts = [(GROUP * g + i, GROUP * (g + 1) + i) for i in range(0, half, 2)]
+                late = jnp.where(rank // GROUP == g, message[1], late) if g else message[1]
                 message = lax.ppermute(message[0], "tm", hosts)
+            if g + 2 == groups:
+                with jax.named_scope("late_slabs"):
+                    late = lax.ppermute(late, "tm", [(i, i + GROUP) for i in range(0, count - GROUP, GROUP)])
+                    late = jnp.where(rank == 0, slabs[2], late)
     with jax.named_scope("spread_results"):
         down = [(i, i + half) for i in range(0, count, 2) if i % GROUP < half]
         pair = lax.ppermute(results[2:], "tm", down)
         pair = jnp.where(place < half, results[:2], pair)
         odd = lax.ppermute(pair[1], "tm", [(i, i + 1) for i in range(0, count, 2)])
-        corrected = jnp.where(core == 0, pair[0], odd)
+        corrected = jnp.where(place == 0, late, jnp.where(core == 0, pair[0], odd))
     return (corrected[None], residual[None])
 
 

time: 196 us -> 194 us (0.990)
  waiting for transfers between devices: 59 us -> 56.2 us
    ppermute x1, waiting for transfers between devices: 37.6 us -> 34.8 us  [shards(): odd = lax.ppermute(pair[1], 'tm', [(i, i + 1) for i in range(0, count, 2)])]
  transfers between devices with their start and end apart: 11 -> 12, of which waited for: 3 -> 3; matrix products, arithmetic and copies ran while one was open for 0% -> 0% of each run, Pallas kernels for 4% -> 4%
where the time goes in v6:
time: 194 us
  waiting for transfers between devices  56.2 us (29%)
  blocking collectives  47.7 us (25%)
  Pallas kernels  45.2 us (23%)
  starting transfers between devices  27.3 us (14%)
  between operations  14.4 us (7%)
  other arithmetic  3.18 us (2%)
    ppermute x1, waiting for transfers between devices, shards(): odd = lax.ppermute(pair[1], 'tm', [(i, i + 1) for i in range(0, count, 2)])  34.8 us
    pallas_call x4, Pallas kernels, run_chain(): pl.pallas_call(functools.partial(chain_kernel, last), out_shape=outs, in_...  30.2 us
    all_gather x1, blocking collectives, shards(): gathered = lax.all_gather(jnp.concatenate([cpoint_guess[0], share]), 'gz')  27.3 us
    all_gather x1, blocking collectives, shards(): initial = lax.all_gather(initial, 'gz')  20.4 us
    all_gather x1, waiting for transfers between devices, shards(): forcing = lax.all_gather(forcing, 'tm', axis_index_groups=members)  20.3 us
    ppermute x1, starting transfers between devices, shards(): piece1 = lax.ppermute(share, 'tm', swap)  8.09 us
    pallas_call x1, Pallas kernels, run_fine(): pl.pallas_call(fine_kernel, out_shape=[f32(NZ, *PLANE), f32(SLAB, *PLANE)...  7.54 us
    pallas_call x1, Pallas kernels, run_start(): pl.pallas_call(start_kernel, out_shape=[f32(NZ, *PLANE), f32(3, SLAB, *PL...  7.5 us
  transfers between devices with their start and end apart: 12, of which 3 were waited for; matrix products, arithmetic and copies ran while one was open for 0% of the time, Pallas kernels for 4%

profile of v6, /device:TPU:57, one launch (start us, length us, event | category | flops | bytes accessed | tf_op | source)
XLA Modules:
  0.0 193.9 jit_solution(12709449645727364089)
XLA Ops:
  7.2 0.0 all-gather.5.cloned.1.call-start
  7.2 0.8 select_select_fusion.2
  8.1 0.8 pad_maximum_fusion
  8.9 27.3 %all-gather = f32[48,32,128]{2,1,0:T(8,128)S(1)} all-gather(f32[6,32,128]{2,1,0:T(8,128)S(1)} %pad_maximum_fusion), channel_id=2, replica_groups=mesh['tm'=64,'gz'=8] {'gz'}, dimensions={0}, use_global_device_ids=true | all-gather | bytes 884736 | tf_op jit(solution)/shard_map/gather_fields/all_gather | solution.py:304
  36.2 3.1 %collective-permute-start.1 = (f32[8,2,32,128]{3,2,1,0:T(8,128)S(1)}, f32[8,2,32,128]{3,2,1,0:T(8,128)S(1)}, u32[]{:S(2)}, u32[]{:S(2)}) collective-permute-start(f32[8,2,32,128]{3,2,1,0:T(8,128)S(1)} %slice.49), channel_id=1, source_target_pairs={{0,16},{8,24},{16,0},{24,8},{32,48},{40,56},{48,32},{56,40},{64,80... | collective-permute-start | bytes 786440 | tf_op jit(solution)/shard_map/share_coefficients/ppermute | solution.py:307
  39.3 8.1 %collective-permute-start = (f32[8,2,32,128]{3,2,1,0:T(8,128)S(1)}, f32[8,2,32,128]{3,2,1,0:T(8,128)S(1)}, u32[]{:S(2)}, u32[]{:S(2)}) collective-permute-start(f32[8,2,32,128]{3,2,1,0:T(8,128)S(1)} %slice.49), channel_id=1, source_target_pairs={{0,8},{8,0},{16,24},{24,16},{32,40},{40,32},{48,56},{56,48},{64,72... | collective-permute-start | bytes 786440 | tf_op jit(solution)/shard_map/share_coefficients/ppermute | solution.py:308
  47.4 4.8 %collective-permute-start.2 = (f32[8,2,32,128]{3,2,1,0:T(8,128)S(1)}, f32[8,2,32,128]{3,2,1,0:T(8,128)S(1)}, u32[]{:S(2)}, u32[]{:S(2)}) collective-permute-start(f32[8,2,32,128]{3,2,1,0:T(8,128)S(1)} %collective-permute-done.1.piece2), channel_id=1, source_target_pairs={{0,8},{8,0},{16,24},{24,16},{32,40},{40,32},{48,56},{56,48},{64,72... | collective-permute-start | bytes 786440 | tf_op jit(solution)/shard_map/share_coefficients/ppermute | solution.py:309
  52.3 0.1 pad_add_fusion.where
  52.4 0.0 collective-permute-done.piece1
  52.4 1.0 collective-permute-done.2.piece3
  53.4 7.5 %fine_spans.1 = (f32[32,32,128]{2,1,0:T(8,128)}, f32[4,32,128]{2,1,0:T(8,128)S(1)}, f32[4,32,128]{2,1,0:T(8,128)S(1)}, f32[8,8,32,128]{3,2,1,0:T(8,128)S(1)}) custom-call(s32[3]{0:T(128)S(1)} %pad_add_fusion.where, f32[8,6,32,128]{3,2,1,0:T(8,128)S(1)} %bitcast.36, f32[8,2,32,128]{3,2,1,0:T(8,128)S(1)} %collective-permute-done.piece1, ...), custom_call_target="tpu_custom_call" | custom-call | flops 42467328 | bytes 94371840 | tf_op jit(solution)/shard_map/fine_spans/pallas_call | solution.py:242
  61.0 0.0 all-gather.5.cloned.1.call-update
  61.0 3.4 %collective-permute-start.4 = (f32[4,32,128]{2,1,0:T(8,128)S(1)}, f32[4,32,128]{2,1,0:T(8,128)S(1)}, u32[]{:S(2)}, u32[]{:S(2)}) collective-permute-start(f32[4,32,128]{2,1,0:T(8,128)S(1)} %get-tuple-element.27), channel_id=1, source_target_pairs={{0,8},{8,16},{16,24},{24,32},{32,40},{40,48},{48,56},{56,64},{64,7... | collective-permute-start | bytes 196616 | tf_op jit(solution)/shard_map/residual/ppermute | solution.py:320
  64.4 3.1 %collective-permute-start.3 = (f32[4,32,128]{2,1,0:T(8,128)S(1)}, f32[4,32,128]{2,1,0:T(8,128)S(1)}, u32[]{:S(2)}, u32[]{:S(2)}) collective-permute-start(f32[4,32,128]{2,1,0:T(8,128)S(1)} %get-tuple-element.26), channel_id=1, source_target_pairs={{0,16},{8,24},{16,32},{24,40},{32,48},{40,56},{48,64},{56,72},{64,... | collective-permute-start | bytes 196616 | tf_op jit(solution)/shard_map/residual/ppermute | solution.py:321
  67.5 20.4 %all-gather.1 = f32[32,32,128]{2,1,0:T(8,128)S(1)} all-gather(f32[4,32,128]{2,1,0:T(8,128)} %param.5), channel_id=3, replica_groups=mesh['tm'=64,'gz'=8] {'gz'}, dimensions={0}, use_global_device_ids=true | all-gather | bytes 589824 | tf_op jit(solution)/shard_map/first_intervals/all_gather | solution.py:317
  87.9 7.5 %first_intervals.1 = (f32[32,32,128]{2,1,0:T(8,128)S(1)}, f32[3,4,32,128]{3,2,1,0:T(8,128)S(1)}) custom-call(s32[3]{0:T(128)S(1)} %pad_add_fusion.where, f32[8,8,32,128]{3,2,1,0:T(8,128)S(1)} %get-tuple-element.21.fields, f32[8,4,32,128]{3,2,1,0:T(8,128)S(1)} %bitcast.37), custom_call_target="tpu_custom_call" | custom-call | flops 47185920 | bytes 104857600 | tf_op jit(solution)/shard_map/first_intervals/pallas_call | solution.py:259
  95.4 0.0 collective-permute-done.4
  95.4 0.7 fusion.4
  96.1 20.3 %all-gather.5.cloned.1.call-done = f32[512,32,128]{2,1,0:T(8,128)} async-done(((f32[32,32,128]{2,1,0:T(8,128)}), f32[512,32,128]{2,1,0:T(8,128)}) %all-gather.5.cloned.1.call-update) | async-done | bytes 8388624 | tf_op jit(solution)/shard_map/gather_forcing/all_gather | solution.py:314
  116.4 7.6 %chain.4 = (f32[32,32,128]{2,1,0:T(8,128)S(1)}, f32[4,32,128]{2,1,0:T(8,128)S(1)}, f32[4,4,32,128]{3,2,1,0:T(8,128)S(1)}) custom-call(s32[3]{0:T(128)S(1)} %pad_add_fusion.where, f32[8,8,32,128]{3,2,1,0:T(8,128)S(1)} %get-tuple-element.21.fields, f32[32,32,128]{2,1,0:T(8,128)S(1)} %get-tuple-element.28.message, f32[16,32,32,128]{3,2,1,0:T(8,128)} %bitcast.38), custom_call_target="tpu_custom_call" | custom-call | flops 37748736 | bytes 83886080 | tf_op jit(solution)/shard_map/chain/pallas_call | solution.py:272
  123.9 0.7 collective-permute-start.5
  124.7 7.6 %chain.5 = (f32[32,32,128]{2,1,0:T(8,128)S(1)}, f32[4,32,128]{2,1,0:T(8,128)S(1)}, f32[4,4,32,128]{3,2,1,0:T(8,128)S(1)}) custom-call(s32[3]{0:T(128)S(1)} %pad_add_fusion.where, f32[8,8,32,128]{3,2,1,0:T(8,128)S(1)} %get-tuple-element.21.fields, f32[32,32,128]{2,1,0:T(8,128)S(1)} %collective-permute-done.5.message, f32[16,32,32,128]{3,2,1,0:T(8,128)} %bitcast.39), custom_call_target="tpu_custom_call" | custom-call | flops 37748736 | bytes 83886080 | tf_op jit(solution)/shard_map/chain/pallas_call | solution.py:272
  132.2 0.7 collective-permute-start.6
  133.0 7.6 %chain.6 = (f32[32,32,128]{2,1,0:T(8,128)S(1)}, f32[4,32,128]{2,1,0:T(8,128)S(1)}, f32[4,4,32,128]{3,2,1,0:T(8,128)S(1)}) custom-call(s32[3]{0:T(128)S(1)} %pad_add_fusion.where, f32[8,8,32,128]{3,2,1,0:T(8,128)S(1)} %get-tuple-element.21.fields, f32[32,32,128]{2,1,0:T(8,128)S(1)} %collective-permute-done.6.message, f32[16,32,32,128]{3,2,1,0:T(8,128)} %bitcast.40), custom_call_target="tpu_custom_call" | custom-call | flops 37748736 | bytes 83886080 | tf_op jit(solution)/shard_map/chain/pallas_call | solution.py:272
  140.5 0.7 collective-permute-start.8
  141.3 7.5 %chain.7 = f32[4,4,32,128]{3,2,1,0:T(8,128)S(1)} custom-call(s32[3]{0:T(128)S(1)} %pad_add_fusion.where, f32[8,8,32,128]{3,2,1,0:T(8,128)S(1)} %get-tuple-element.21.fields, f32[32,32,128]{2,1,0:T(8,128)S(1)} %collective-permute-done.8.message, f32[16,32,32,128]{3,2,1,0:T(8,128)} %bitcast.41), custom_call_target="tpu_custom_call" | custom-call | flops 37748736 | bytes 83886080 | tf_op jit(solution)/shard_map/chain/pallas_call | solution.py:272
  148.8 0.1 select_select_fusion
  148.9 0.7 collective-permute-start.9
  149.6 0.7 collective-permute-start.7
  150.3 1.3 collective-permute-start.10
  151.6 34.8 %collective-permute-done.10 = f32[4,32,128]{2,1,0:T(8,128)S(1)} collective-permute-done((f32[4,32,128]{2,1,0:T(8,128)S(1)}, f32[4,32,128]{2,1,0:T(8,128)S(1)}, u32[]{:S(2)}, u32[]{:S(2)}) %collective-permute-start.10) | collective-permute-done | bytes 65568 | tf_op jit(solution)/shard_map/spread_results/ppermute | solution.py:348
  186.4 0.6 fusion.2
  (12 shorter events, 0.1 us)
Async XLA Ops:
  7.2 109.2 %all-gather.5.cloned.1.call-start = ((), (), s32[]{:S(2)}) async-start(), calls=%async_computation | async-start | bytes 8912896 | tf_op jit(solution)/shard_map/gather_forcing/all_gather | solution.py:314
  36.2 11.2 %collective-permute-start.1 = (f32[8,2,32,128]{3,2,1,0:T(8,128)S(1)}, f32[8,2,32,128]{3,2,1,0:T(8,128)S(1)}, u32[]{:S(2)}, u32[]{:S(2)}) collective-permute-start(f32[8,2,32,128]{3,2,1,0:T(8,128)S(1)} %slice.49), channel_id=1, source_target_pairs={{0,16},{8,24},{16,0},{24,8},{32,48},{40,56},{48,32},{56,40},{64,80... | collective-permute-start | bytes 786440 | tf_op jit(solution)/shard_map/share_coefficients/ppermute | solution.py:307
  39.3 13.0 %collective-permute-start = (f32[8,2,32,128]{3,2,1,0:T(8,128)S(1)}, f32[8,2,32,128]{3,2,1,0:T(8,128)S(1)}, u32[]{:S(2)}, u32[]{:S(2)}) collective-permute-start(f32[8,2,32,128]{3,2,1,0:T(8,128)S(1)} %slice.49), channel_id=1, source_target_pairs={{0,8},{8,0},{16,24},{24,16},{32,40},{40,32},{48,56},{56,48},{64,72... | collective-permute-start | bytes 786440 | tf_op jit(solution)/shard_map/share_coefficients/ppermute | solution.py:308
  47.4 6.0 %collective-permute-start.2 = (f32[8,2,32,128]{3,2,1,0:T(8,128)S(1)}, f32[8,2,32,128]{3,2,1,0:T(8,128)S(1)}, u32[]{:S(2)}, u32[]{:S(2)}) collective-permute-start(f32[8,2,32,128]{3,2,1,0:T(8,128)S(1)} %collective-permute-done.1.piece2), channel_id=1, source_target_pairs={{0,8},{8,0},{16,24},{24,16},{32,40},{40,32},{48,56},{56,48},{64,72... | collective-permute-start | bytes 786440 | tf_op jit(solution)/shard_map/share_coefficients/ppermute | solution.py:309
  61.0 34.4 %collective-permute-start.4 = (f32[4,32,128]{2,1,0:T(8,128)S(1)}, f32[4,32,128]{2,1,0:T(8,128)S(1)}, u32[]{:S(2)}, u32[]{:S(2)}) collective-permute-start(f32[4,32,128]{2,1,0:T(8,128)S(1)} %get-tuple-element.27), channel_id=1, source_target_pairs={{0,8},{8,16},{16,24},{24,32},{32,40},{40,48},{48,56},{56,64},{64,7... | collective-permute-start | bytes 196616 | tf_op jit(solution)/shard_map/residual/ppermute | solution.py:320
  64.4 31.0 %collective-permute-start.3 = (f32[4,32,128]{2,1,0:T(8,128)S(1)}, f32[4,32,128]{2,1,0:T(8,128)S(1)}, u32[]{:S(2)}, u32[]{:S(2)}) collective-permute-start(f32[4,32,128]{2,1,0:T(8,128)S(1)} %get-tuple-element.26), channel_id=1, source_target_pairs={{0,16},{8,24},{16,32},{24,40},{32,48},{40,56},{48,64},{56,72},{64,... | collective-permute-start | bytes 196616 | tf_op jit(solution)/shard_map/residual/ppermute | solution.py:321
  123.9 0.7 collective-permute-start.5
  132.2 0.7 collective-permute-start.6
  140.5 0.7 collective-permute-start.8
  148.9 1.4 collective-permute-start.9
  149.6 2.0 %collective-permute-start.7 = (f32[4,32,128]{2,1,0:T(8,128)S(1)}, f32[4,32,128]{2,1,0:T(8,128)S(1)}, u32[]{:S(2)}, u32[]{:S(2)}) collective-permute-start(f32[4,32,128]{2,1,0:T(8,128)S(1)} %select_select_fusion.1), channel_id=1, source_target_pairs={{0,128},{128,256},{256,384},{1,129},{129,257},{257,385},{2,130},{1... | collective-permute-start | bytes 196616 | tf_op jit(solution)/shard_map/late_slabs/ppermute | solution.py:342
  150.3 36.1 %collective-permute-start.10 = (f32[4,32,128]{2,1,0:T(8,128)S(1)}, f32[4,32,128]{2,1,0:T(8,128)S(1)}, u32[]{:S(2)}, u32[]{:S(2)}) collective-permute-start(f32[4,32,128]{2,1,0:T(8,128)S(1)} %slice_bitcast_fusion), channel_id=1, source_target_pairs={{0,8},{16,24},{32,40},{48,56},{64,72},{80,88},{96,104},{112,120},{... | collective-permute-start | bytes 196616 | tf_op jit(solution)/shard_map/spread_results/ppermute | solution.py:348
Sparse Core Ops, SparseCore 0:
  61.1 55.2 all-gather.4
